TPU v7x, 128 devices: a whole 4x4x4 slice. The times are simulated.
128 devices in a mesh: pitch: 8 (over y, core), span: 16 (over x, z).
Axes of the slice: x: 4, y: 4, z: 4, core: 2. Of those that a mesh axis runs over, the one named last changes fastest.
Arguments:
- flow_state: float32 [4, 256, 1024, 256], P(None, 'pitch', 'span'), may hold values from -6 to 6
- wall_inverse: float32 [64, 64], replicated, as said below
- metal_inverse: float32 [16, 16], replicated, as said below
- metal_state: float32 [16, 262144], P(None, ('pitch', 'span')), may hold values from -6 to 6
- metal_conduct: float32 [262144], P(('pitch', 'span')), may hold values from 0.3 to 3
- face_coef: float32 [2, 131072], P(None, ('pitch', 'span')), may hold values from 0.3 to 3
- owner_map: int32 [131072, 1], P(('pitch', 'span')), may hold values from 0 to 127; in each aligned block of 1024 rows (0 to 1023, 1024 to 2047, ...) at most 16 rows name the same one
- face_cell: int32 [131072], P(('pitch', 'span')), may hold values from 0 to 2047
- sample_col: int32 [131072], P(('pitch', 'span')), may hold values from 0 to 2047
- sample_low: int32 [131072], P(('pitch', 'span')), may hold values from 0 to 192
Outputs:
- new_state: float32 [4, 256, 1024, 256], P(None, 'pitch', 'span')
- metal_out: float32 [16, 262144], P(None, ('pitch', 'span'))
Inputs may be any that keep to these rules, and one draw needn't show every extreme that they name: `owner_map`: at most 16 faces of one device have the same owner; in every draw some device sends exactly 16 faces to one owner. `face_cell`: columns are numbered pitch cell times 64 plus span cell. `sample_col`: numbered as face_cell. `wall_inverse`: diagonal entries are the largest of their rows, within 0.5 to 1. `metal_inverse`: diagonal entries are the largest of their rows, within 0.5 to 1.
All inputs are finite; a program needn't handle non-finite values.
Results may differ from a plain program's by a relative error of at most 0.0001.
Values sent between devices are 32-bit elements; how exact they have to be, the bound alone decides.
No kernel may reach another device: no remote copies, remote signals or barrier semaphores. Data moves between devices by JAX's collectives and lax.ppermute only.
A program may use at most 128 MiB of HBM per device.

v0:
```python
import jax
import jax.numpy as jnp
from jax import lax
from jax.experimental import pallas as pl
from jax.experimental.pallas import tpu as pltpu
from jax.sharding import PartitionSpec as P

CP = 32
CS = 64
GN = 256
WM = 64
MP = 16
CAP = 16
DEV = 128
FACES = 1024
SLOT_DEV = 2048
COLS = CP * CS
PICARD = 3

F32 = jnp.float32
BF16 = jnp.bfloat16
I32 = jnp.int32
AXES = ("pitch", "span")
VMEM_LIMIT = 48 * 1024 * 1024
VMEM_WHOLE = 60 * 1024 * 1024
FB = 256
PAD = 8


def iota(shape, dim):
    return lax.broadcasted_iota(I32, shape, dim)


def dot_nn(a, b):
    return lax.dot_general(a, b, (((1,), (0,)), ((), ())), preferred_element_type=F32)


def dot_nt(a, b):
    return lax.dot_general(a, b, (((1,), (1,)), ((), ())), preferred_element_type=F32)


def split2(x):
    hi = x.astype(BF16).astype(F32)
    return hi, x - hi


def split3(x):
    hi = x.astype(BF16).astype(F32)
    rest = x - hi
    mid = rest.astype(BF16).astype(F32)
    return hi, mid, rest - mid


def cast(x):
    return x.astype(BF16)


def cell_tables(cell_row):
    width = cell_row.shape[1]
    span_hot = iota((CS, width), 0) == (cell_row & (CS - 1))
    pitch_hot = iota((CP, width), 0) == (cell_row >> 6)
    return jnp.where(span_hot, 1.0, 0.0), pitch_hot


def gather_lane(source, index):
    return jnp.take_along_axis(source, index, axis=1)


def pick_rows(refs, col_ref, base):
    sub = iota((8, 128), 0)
    blocks = [None] * len(refs)
    for i in range(8):
        at = col_ref[base + i]
        for k, ref in enumerate(refs):
            row = jnp.broadcast_to(ref[pl.ds(at, 1), :], (8, 128))
            blocks[k] = row if i == 0 else jnp.where(sub == i, row, blocks[k])
    return blocks


def first_kernel(
    state, *args,
):
    sources, (send, first_p, last_p, first_s, last_s, rank, top, free, walls) = args[:9], args[9:18]
    cur, lowb, temp, force, out_send, edge_p, edge_s, sems, *held = args[18:]
    col, low, owner, coef, cell, wall_inv, metal_inv, metal, conduct = held
    small = [
        pltpu.make_async_copy(source, target, sems.at[9 + (i == 0)])
        for i, (source, target) in enumerate(zip(sources, held))
    ]
    for copy in small:
        copy.start()
    columns = state.reshape(4, COLS, GN)
    loads = []
    for i, c in enumerate((2, 0, 1, 3)):
        for h in range(2):
            loads.append(
                pltpu.make_async_copy(
                    columns.at[c, :, pl.ds(128 * h, 128)],
                    cur.at[2 * c + h, pl.ds(0, COLS)],
                    sems.at[i],
                )
            )
    for copy in loads:
        copy.start()
    edges_in = [
        pltpu.make_async_copy(state.at[:, 0], edge_p.at[0], sems.at[4]),
        pltpu.make_async_copy(state.at[:, CP - 1], edge_p.at[1], sems.at[5]),
    ]
    for copy in edges_in:
        copy.start()

    for copy in small[1:]:
        copy.wait()

    eye = iota((128, 128), 0) == iota((128, 128), 1)
    ones = jnp.ones((128, 128), BF16)
    low_f = low[...].astype(F32)
    for b in range(FACES // 128):
        diag = jnp.where(eye, low_f[:, 128 * b : 128 * (b + 1)], 0.0)
        lowb[pl.ds(128 * b, 128), :] = dot_nn(cast(diag), ones).astype(I32)

    m = metal[...]
    inv = metal_inv[...]
    v = inv[:, 0:1] * m[0:1, :]
    for j in range(1, MP):
        v = v + inv[:, j : j + 1] * m[j : j + 1, :]
    free[...] = v
    v0 = jnp.concatenate([v[0:1, 128 * g : 128 * (g + 1)] for g in range(16)], axis=0)
    spread = jnp.where((iota((DEV, 16), 0) >> 3) == iota((DEV, 16), 1), 1.0, 0.0)
    parts = jnp.concatenate(split3(v0) + split3(conduct[...]), axis=1)
    wide = dot_nn(cast(spread), cast(parts))
    lane = iota((DEV, 128), 1)
    mine = (lane >> 4) == (iota((DEV, 128), 0) & 7)
    folded = []
    for k in range(2):
        a = wide[:, 384 * k : 384 * (k + 1)]
        y = jnp.where(mine, a[:, 0:128] + a[:, 128:256] + a[:, 256:384], 0.0)
        for step in (64, 32, 16):
            y = y + pltpu.roll(y, step, 1)
        folded.append(y)
    own_half = jnp.where(lane < 16, folded[0], folded[1])

    before = jnp.where(iota((FB, FB), 0) < iota((FB, FB), 1), 1.0, 0.0).astype(BF16)
    carry = jnp.zeros((DEV, 1), F32)
    for b in range(FACES // FB):
        cols = slice(FB * b, FB * (b + 1))
        hot = jnp.where(iota((DEV, FB), 0) == owner[:, cols], 1.0, 0.0)
        prior = dot_nn(cast(hot), before) + carry
        carry = carry + jnp.sum(hot, axis=1, keepdims=True)
        rank[:, cols] = jnp.sum(hot * prior, axis=0, keepdims=True).astype(I32)

    for copy in edges_in:
        copy.wait()
    edges_out = [
        pltpu.make_async_copy(edge_p.at[0], first_p, sems.at[4]),
        pltpu.make_async_copy(edge_p.at[1], last_p, sems.at[5]),
    ]
    for copy in edges_out:
        copy.start()
    small[0].wait()
    for copy in loads[0:6]:
        copy.wait()
    halves = [[cur.at[2 * c + h] for h in range(2)] for c in range(4)]
    lane8 = iota((8, 128), 1)
    left = lane8 < WM

    def body(g, _):
        base = g * 8
        index = lowb[pl.ds(base, 8), :] + (lane8 & (WM - 1))
        near = index < 128
        index = index & 127
        found = pick_rows([halves[c][h] for c in range(3) for h in range(2)], col, base)
        found = [gather_lane(x, index) for x in found]
        picked = [jnp.where(near, found[2 * c], found[2 * c + 1]) for c in range(3)]
        force[pl.ds(base, 8), :] = jnp.where(left, picked[0], picked[1])
        temp[pl.ds(base, 8), :] = picked[2]
        return 0

    lax.fori_loop(0, FACES // 8, body, 0, unroll=8)

    g = wall_inv[...]
    g_hi, g_lo = split2(g)
    top_hi, top_lo = g_hi[0:1, :], g_lo[0:1, :]
    none = jnp.zeros((1, WM), F32)
    row16 = iota((16, 128), 0)
    query = jnp.where(
        row16 == 0,
        jnp.concatenate([top_hi, top_hi], axis=1),
        jnp.where(row16 == 1, jnp.concatenate([top_lo, none], axis=1), 0.0),
    )
    total = jnp.zeros((DEV, 128), F32)
    left_b = iota((FB, 128), 1) < WM
    for b in range(FACES // FB):
        cols = slice(FB * b, FB * (b + 1))
        x_hi, x_lo = split2(temp[cols, :])
        p = dot_nt(cast(query), cast(jnp.where(left_b, x_hi, x_lo)))
        p = p[0:1, :] + p[1:2, :]
        top[:, cols] = p
        hot = jnp.where(iota((DEV, FB), 0) == owner[:, cols], 1.0, 0.0)
        which = iota((CAP, FB), 0) == rank[:, cols]
        kf_parts = split3(coef[0:1, cols])
        p_parts = split3(p)
        pieces = [jnp.zeros((32, FB), F32)]
        for kf_part, p_part in zip(kf_parts, p_parts):
            pieces.append(jnp.where(which, kf_part, 0.0))
            pieces.append(jnp.where(which, p_part, 0.0))
        total = total + dot_nt(cast(hot), cast(jnp.concatenate(pieces, axis=0)))
    total = total + pltpu.roll(total, 96, 1) + pltpu.roll(total, 64, 1)
    out_send[...] = jnp.where(lane < 32, own_half, jnp.where(lane < 64, total, 0.0))
    give = [pltpu.make_async_copy(out_send, send, sems.at[6])]
    give[0].start()

    for copy in loads[6:]:
        copy.wait()
    for c in range(4):
        for h in range(2):
            lanes = slice(128 * h, 128 * h + 128)
            for p in range(0, CP, 8):
                edge_s[0, c, p : p + 8, lanes] = halves[c][h][pl.ds(p * CS, 8, stride=CS), :]
                edge_s[1, c, p : p + 8, lanes] = halves[c][h][
                    pl.ds(p * CS + CS - 1, 8, stride=CS), :
                ]
    give.append(pltpu.make_async_copy(edge_s.at[0], first_s, sems.at[7]))
    give.append(pltpu.make_async_copy(edge_s.at[1], last_s, sems.at[8]))
    give[1].start()
    give[2].start()

    blank = jnp.zeros((WM, WM), F32)

    def twice(part):
        return jnp.concatenate(
            [
                jnp.concatenate([part, blank], axis=1),
                jnp.concatenate([blank, part], axis=1),
            ],
            axis=0,
        )

    both_hi = jnp.transpose(twice(g_hi))
    both_lo = jnp.transpose(twice(g_lo))
    table = cast(
        jnp.concatenate(
            [
                jnp.concatenate([both_hi, both_lo], axis=1),
                jnp.concatenate([both_hi, jnp.zeros_like(both_lo)], axis=1),
            ],
            axis=0,
        )
    )
    row16 = iota((16, 256), 0)
    picks = (
        jnp.concatenate([top_hi, none, top_hi, none], axis=1),
        jnp.concatenate([none, top_hi, none, top_hi], axis=1),
        jnp.concatenate([top_lo, none, none, none], axis=1),
        jnp.concatenate([none, top_lo, none, none], axis=1),
    )
    query = jnp.zeros((16, 256), F32)
    for i, pick in enumerate(picks):
        query = jnp.where(row16 == i, pick, query)
    query = cast(query)

    def packed(x):
        hi, lo = split2(x)
        return cast(jnp.concatenate([hi, lo], axis=1))

    blocks = [slice(FB * b, FB * (b + 1)) for b in range(FACES // FB)]
    ys = [dot_nn(packed(force[cols, :]), table) for cols in blocks]
    for step in range(PICARD):
        rhs = []
        for cols, y in zip(blocks, ys):
            x = y[:, :128] + y[:, 128:]
            sq = x * x
            damping = 0.5 * lax.rsqrt(1.0 + sq + pltpu.roll(sq, WM, 1))
            rhs.append(packed(force[cols, :] - damping * x))
        if step < PICARD - 1:
            ys = [dot_nn(r, table) for r in rhs]
        else:
            ys = [dot_nt(query, r) for r in rhs]
    total = jnp.zeros((CS, 192), F32)
    for cols, y in zip(blocks, ys):
        nu = coef[1:2, cols]
        flux_u = nu * (y[0:1, :] + y[2:3, :])
        flux_w = nu * (y[1:2, :] + y[3:4, :])
        span_hot, pitch_hot = cell_tables(cell[:, cols])
        pieces = []
        for u_part, w_part in zip(split3(flux_u), split3(flux_w)):
            pieces.append(jnp.where(pitch_hot, u_part, 0.0))
            pieces.append(jnp.where(pitch_hot, w_part, 0.0))
        total = total + dot_nt(cast(span_hot), cast(jnp.concatenate(pieces, axis=0)))
    walls[...] = jnp.zeros((CS, 128), F32)
    walls[:, 0:64] = -0.5 * (total[:, 0:64] + total[:, 64:128] + total[:, 128:192])
    for copy in edges_out + give:
        copy.wait()


GROUP = 4
HALO = 8
ROWS = CS + 2 * HALO


def stencil_kernel(state, walls, prev_p, next_p, prev_s, next_s, out, kept, cur, work, sems):
    inner = pl.ds(HALO, CS)
    loads = []
    for c in range(4):
        for h in range(2):
            lanes = pl.ds(128 * h, 128)
            loads.append(
                pltpu.make_async_copy(
                    state.at[c, :, :, lanes], cur.at[h, c, pl.ds(1, CP), inner, :], sems.at[c]
                )
            )
            if c == 0:
                for plane, source in ((0, prev_p), (CP + 1, next_p)):
                    loads.append(
                        pltpu.make_async_copy(
                            source.at[:, :, lanes], cur.at[h, :, plane, inner, :], sems.at[4]
                        )
                    )
    for copy in loads:
        copy.start()

    flat = cur.reshape(2 * 4 * (CP + 2) * ROWS, 128)
    for h in range(2):
        lanes = slice(128 * h, 128 * h + 128)
        for c in range(4):
            for p in range(0, CP, 8):
                start = ((h * 4 + c) * (CP + 2) + 1 + p) * ROWS
                flat[pl.ds(start + HALO - 1, 8, stride=ROWS), :] = prev_s[c, p : p + 8, lanes]
                flat[pl.ds(start + HALO + CS, 8, stride=ROWS), :] = next_s[c, p : p + 8, lanes]

    i, j = iota((GN, GN), 0), iota((GN, GN), 1)
    near = jnp.where(jnp.abs(i - j) == 1, 1.0, 0.0)
    same = jnp.where((i == 0) | (i == GN - 1), 5.0, 4.0)
    matrix = jnp.where(i == j, same, near)
    matrix = cast(jnp.concatenate([matrix, matrix], axis=0))
    first_lane = iota((CS, 128), 1) == 0

    def put(c, h):
        lanes = pl.ds(128 * h, 128)
        return pltpu.make_async_copy(work.at[h, c], out.at[c, :, :, lanes], sems.at[5 + c])

    for copy in loads[0:6]:
        copy.wait()
    for c in range(4):
        if c > 0:
            loads[4 + 2 * c].wait()
            loads[5 + 2 * c].wait()

        def body(n, _):
            p = n * GROUP
            split = []
            for q in range(GROUP):
                a = cur[0, c, p + 1 + q, HALO : HALO + CS, :]
                b = cur[1, c, p + 1 + q, HALO : HALO + CS, :]
                a_hi, a_lo = split2(a)
                b_hi, b_lo = split2(b)
                split.append(jnp.concatenate([cast(x) for x in (a_hi, b_hi, a_lo, b_lo)], axis=1))
            y = dot_nn(jnp.concatenate(split, axis=0), matrix)
            for q in range(GROUP):
                for h in range(2):
                    up = cur[h, c, p + 1 + q, HALO + 1 : HALO + CS + 1, :]
                    dn = cur[h, c, p + 1 + q, HALO - 1 : HALO + CS - 1, :]
                    after = cur[h, c, p + 2 + q, HALO : HALO + CS, :]
                    prior = cur[h, c, p + q, HALO : HALO + CS, :]
                    mid = y[CS * q : CS * (q + 1), 128 * h : 128 * (h + 1)]
                    value = 0.1 * (mid + (up + dn)) + (0.25 * prior - 0.05 * after)
                    if c < 2 and h == 0:
                        wall = pltpu.roll(walls[...], 128 - (c * CP + p + q), 1)
                        value = value + jnp.where(first_lane, wall, 0.0)
                    if c == 2 and h == 0:
                        kept[p + q, :, :] = value
                    else:
                        work[h, c, p + q, :, :] = value
            return 0

        lax.fori_loop(0, CP // GROUP, body, 0)
        for h in range(2):
            if c != 2 or h == 1:
                put(c, h).start()
    for c in range(4):
        for h in range(2):
            if c != 2 or h == 1:
                put(c, h).wait()


def last_kernel(
    state, kept, recv, send, free, metal, owner, rank, top, coef, cell, wall_inv, metal_inv,
    out, metal_out,
    sems,
):
    corner_f = 0.5 * wall_inv[0:1, 0:1]
    corner_m = 0.5 * metal_inv[0:1, 0:1]
    got = recv[...]
    from_owner = jnp.transpose(got)[0:32, :]
    parts = cast(jnp.concatenate(split3(from_owner), axis=0))
    total = jnp.zeros((CS, 96), F32)
    for b in range(FACES // FB):
        cols = slice(FB * b, FB * (b + 1))
        hot = jnp.where(iota((DEV, FB), 0) == owner[:, cols], 1.0, 0.0)
        y = dot_nn(parts, cast(hot))
        y = y[0:32, :] + y[32:64, :] + y[64:96, :]
        which = iota((CAP, FB), 0) == rank[:, cols]
        v0 = jnp.sum(jnp.where(which, y[0:16, :], 0.0), axis=0, keepdims=True)
        km = jnp.sum(jnp.where(which, y[16:32, :], 0.0), axis=0, keepdims=True)
        kf = coef[0:1, cols]
        p = top[:, cols]
        tw = (kf * p + km * v0) / (kf * (1.0 - corner_f) + km * (1.0 - corner_m))
        heat = kf * (p + (corner_f - 1.0) * tw)
        span_hot, pitch_hot = cell_tables(cell[:, cols])
        pieces = [jnp.where(pitch_hot, part, 0.0) for part in split3(heat)]
        total = total + dot_nt(cast(span_hot), cast(jnp.concatenate(pieces, axis=0)))
    wall = -0.5 * (total[:, 0:32] + total[:, 32:64] + total[:, 64:96])
    wall = jnp.concatenate([wall, jnp.zeros((CS, 96), F32)], axis=1)
    first_lane = iota((CS, 128), 1) == 0
    for p in range(CP):
        column = wall if p == 0 else pltpu.roll(wall, 128 - p, 1)
        kept[p] = kept[p] + jnp.where(first_lane, column, 0.0)
    copy = pltpu.make_async_copy(kept, out.at[2, :, :, pl.ds(0, 128)], sems.at[0])
    copy.start()

    own = send[...]
    lane = iota((DEV, 128), 1)
    kf = pltpu.roll(got, 96, 1)
    p = pltpu.roll(got, 80, 1)
    km = pltpu.roll(own, 112, 1)
    valid = lane < CAP
    tw = (kf * p + km * own) / jnp.where(valid, kf * (1.0 - corner_f) + km * (1.0 - corner_m), 1.0)
    tw = jnp.where(valid, tw, 0.0)
    used = jnp.where(jnp.logical_and(valid, kf > 0.0), 1.0, 0.0)
    for step in (16, 32, 64):
        tw = tw + pltpu.roll(tw, step, 1)
        used = used + pltpu.roll(used, step, 1)
    mine = (lane >> 4) == (iota((DEV, 128), 0) & 7)
    tw = jnp.where(mine, tw, 0.0)
    used = jnp.where(mine, used, 0.0)
    gain = 0.5 * metal_inv[:, 0:1]
    for g in range(16):
        rows = slice(8 * g, 8 * g + 8)
        cols = slice(128 * g, 128 * g + 128)
        tw_row = jnp.sum(tw[rows, :], axis=0, keepdims=True)
        used_row = jnp.sum(used[rows, :], axis=0, keepdims=True)
        metal_out[:, cols] = jnp.where(
            used_row > 0.5, free[:, cols] + gain * tw_row, metal[:, cols]
        )
    copy.wait()


def spec(space):
    return pl.BlockSpec(memory_space=space)


ANY = pl.ANY
VM = pltpu.VMEM
HBM = pltpu.HBM


def shape(dims, dtype=F32):
    return jax.ShapeDtypeStruct(dims, dtype)


def params(limit=VMEM_LIMIT):
    return pltpu.CompilerParams(vmem_limit_bytes=limit)


def cost(microseconds):
    return pl.CostEstimate(
        flops=0, bytes_accessed=int(microseconds * 3_000_000), transcendentals=0
    )


def local(
    flow_state,
    wall_inverse,
    metal_inverse,
    metal_state,
    metal_conduct,
    face_coef,
    owner_map,
    face_cell,
    sample_col,
    sample_low,
):
    owner = owner_map.reshape(1, FACES)
    cell = face_cell.reshape(1, FACES)
    low = sample_low.reshape(1, FACES)
    conduct = metal_conduct.reshape(16, 128)
    send, first_p, last_p, first_s, last_s, rank, top, free, walls = pl.pallas_call(
        first_kernel,
        name="first",
        in_specs=[spec(HBM)] * 10,
        out_specs=[spec(ANY)] * 5 + [spec(VM)] * 4,
        out_shape=[
            shape((DEV, 128)),
            shape((4, CS, GN)),
            shape((4, CS, GN)),
            shape((4, CP, GN)),
            shape((4, CP, GN)),
            shape((1, FACES), I32),
            shape((1, FACES)),
            shape((MP, SLOT_DEV)),
            shape((CS, 128)),
        ],
        scratch_shapes=[
            pltpu.VMEM((8, COLS + PAD, 128), F32),
            pltpu.VMEM((FACES, 128), I32),
            pltpu.VMEM((FACES, 128), F32),
            pltpu.VMEM((FACES, 128), F32),
            pltpu.VMEM((DEV, 128), F32),
            pltpu.VMEM((2, 4, CS, GN), F32),
            pltpu.VMEM((2, 4, CP, GN), F32),
            pltpu.SemaphoreType.DMA((11,)),
            pltpu.SMEM((FACES,), I32),
            pltpu.VMEM((1, FACES), I32),
            pltpu.VMEM((1, FACES), I32),
            pltpu.VMEM((2, FACES), F32),
            pltpu.VMEM((1, FACES), I32),
            pltpu.VMEM((WM, WM), F32),
            pltpu.VMEM((MP, MP), F32),
            pltpu.VMEM((MP, SLOT_DEV), F32),
            pltpu.VMEM((16, 128), F32),
        ],
        compiler_params=params(VMEM_WHOLE),
        cost_estimate=cost(7),
    )(
        flow_state, sample_col, low, owner, face_coef, cell, wall_inverse, metal_inverse,
        metal_state, conduct,
    )

    recv = lax.all_to_all(send, AXES, split_axis=0, concat_axis=0, tiled=True)

    n_pitch, n_span = lax.axis_size("pitch"), lax.axis_size("span")
    up_p = [(i, (i + 1) % n_pitch) for i in range(n_pitch)]
    up_s = [(i, i + 1) for i in range(n_span - 1)]
    prev_p = lax.ppermute(last_p, "pitch", up_p)
    next_p = lax.ppermute(first_p, "pitch", [(j, i) for i, j in up_p])
    prev_s = lax.ppermute(last_s, "span", up_s)
    next_s = lax.ppermute(first_s, "span", [(j, i) for i, j in up_s])

    new_state, kept = pl.pallas_call(
        stencil_kernel,
        name="stencil",
        in_specs=[spec(ANY), spec(VM), spec(ANY), spec(ANY), spec(VM), spec(VM)],
        out_specs=[spec(ANY), spec(VM)],
        out_shape=[shape((4, CP, CS, GN)), shape((CP, CS, 128))],
        scratch_shapes=[
            pltpu.VMEM((2, 4, CP + 2, ROWS, 128), F32),
            pltpu.VMEM((2, 4, CP, CS, 128), F32),
            pltpu.SemaphoreType.DMA((9,)),
        ],
        compiler_params=params(),
        cost_estimate=cost(8),
    )(flow_state, walls, prev_p, next_p, prev_s, next_s)

    new_state, metal_out = pl.pallas_call(
        last_kernel,
        name="last",
        in_specs=[spec(ANY)] + [spec(VM)] * 12,
        out_specs=[spec(ANY), spec(VM)],
        out_shape=[shape((4, CP, CS, GN)), shape((MP, SLOT_DEV))],
        input_output_aliases={0: 0},
        scratch_shapes=[pltpu.SemaphoreType.DMA((1,))],
        compiler_params=params(),
        cost_estimate=cost(3),
    )(
        new_state, kept, recv, send, free, metal_state, owner, rank, top, face_coef, cell,
        wall_inverse, metal_inverse,
    )
    return (new_state, metal_out)


def solution(mesh):
    return jax.shard_map(
        local,
        mesh=mesh,
        in_specs=(
            P(None, "pitch", "span", None),
            P(),
            P(),
            P(None, ("pitch", "span")),
            P(("pitch", "span")),
            P(None, ("pitch", "span")),
            P(("pitch", "span"), None),
            P(("pitch", "span")),
            P(("pitch", "span")),
            P(("pitch", "span")),
        ),
        out_specs=(P(None, "pitch", "span", None), P(None, ("pitch", "span"))),
        check_vma=False,
    )
```

profile of v0, /device:TPU:1, one launch (start us, length us, event | category | flops | bytes accessed | tf_op | source)
XLA Modules:
  0.0 44.4 jit_solution(5385153812305485467)
XLA Ops:
  0.7 10.3 %first.1 = (f32[128,128]{1,0:T(8,128)}, f32[4,64,256]{2,1,0:T(8,128)}, f32[4,64,256]{2,1,0:T(8,128)}, f32[4,32,256]{2,1,0:T(8,128)}, f32[4,32,256]{2,1,0:T(8,128...) custom-call(f32[4,32,64,256]{3,2,1,0:T(8,128)} %state.3, s32[1024]{0:T(1024)} %args_0_.4, ...), custom_call_target="tpu_custom_call" | custom-call | bytes 21000000 | tf_op jit(solution)/shard_map/first/pallas_call | solution.py:487
  11.0 2.7 %collective-permute-start = (f32[4,64,256]{2,1,0:T(8,128)}, f32[4,64,256]{2,1,0:T(8,128)S(1)}, u32[]{:S(2)}, u32[]{:S(2)}) collective-permute-start(f32[4,64,256]{2,1,0:T(8,128)} %get-tuple-element.14), channel_id=1, source_target_pairs={{0,16},{16,32},{32,48},{48,64},{64,80},{80,96},{96,112},{112,0},{1... | collective-permute-start | bytes 786440 | tf_op jit(solution)/shard_map/ppermute | solution.py:534
  13.7 0.0 collective-permute-start.1
  13.7 3.5 %collective-permute-start.2 = (f32[4,32,256]{2,1,0:T(8,128)}, f32[4,32,256]{2,1,0:T(8,128)S(1)}, u32[]{:S(2)}, u32[]{:S(2)}) collective-permute-start(f32[4,32,256]{2,1,0:T(8,128)} %get-tuple-element.16), channel_id=1, source_target_pairs={{0,1},{1,2},{2,3},{3,4},{4,5},{5,6},{6,7},{7,8},{8,9},{9,10},{10,1... | collective-permute-start | bytes 393224 | tf_op jit(solution)/shard_map/ppermute | solution.py:536
  17.2 1.3 %collective-permute-start.3 = (f32[4,32,256]{2,1,0:T(8,128)}, f32[4,32,256]{2,1,0:T(8,128)S(1)}, u32[]{:S(2)}, u32[]{:S(2)}) collective-permute-start(f32[4,32,256]{2,1,0:T(8,128)} %get-tuple-element.17), channel_id=1, source_target_pairs={{1,0},{2,1},{3,2},{4,3},{5,4},{6,5},{7,6},{8,7},{9,8},{10,9},{11,1... | collective-permute-start | bytes 393224 | tf_op jit(solution)/shard_map/ppermute | solution.py:537
  18.5 11.6 %all-to-all-start = ((f32[128,1,128]{2,1,0:T(1,128)}), f32[128,1,128]{2,1,0:T(1,128)S(1)}, u32[]{:S(2)}, u32[]{:S(2)}) async-start(f32[128,1,128]{2,1,0:T(1,128)} %bitcast.8), calls=%async_computation | async-start | bytes 131072 | tf_op jit(solution)/shard_map/all_to_all | solution.py:529
  30.1 0.0 collective-permute-done.2.prev_s
  30.1 0.0 collective-permute-done.3.next_s
  30.1 0.0 collective-permute-done.prev_p
  30.1 0.0 collective-permute-done.1.next_p
  30.2 0.7 %copy-done.4 = f32[64,128]{1,0:T(8,128)S(1)} copy-done((f32[64,128]{1,0:T(8,128)S(1)}, f32[64,128]{1,0:T(8,128)}, u32[]{:S(2)}) %copy-start.4) | copy-done | bytes 32792
  30.9 10.7 %stencil.1 = (f32[4,32,64,256]{3,2,1,0:T(8,128)}, f32[32,64,128]{2,1,0:T(8,128)S(1)}) custom-call(f32[4,32,64,256]{3,2,1,0:T(8,128)} %state.3, f32[64,128]{1,0:T(8,128)S(1)} %copy-done.4, f32[4,64,256]{2,1,0:T(8,128)S(1)} %collective-permute-done.prev_p, f32[4,64,256]{2,1,0:T(8,128)S(1)} %collective-permute-done.1.next_p, ...), custom_call_target="tpu_custom_call" | custom-call | bytes 24000000 | tf_op jit(solution)/shard_map/stencil/pallas_call | solution.py:539
  41.6 0.0 all-to-all-done
  41.6 0.0 copy-done
  41.6 0.0 copy-done.3
  41.6 0.0 copy-done.5
  41.6 0.0 copy-done.6
  41.7 0.0 copy-done.7
  41.7 0.0 copy-done.8
  41.7 0.0 copy-done.1
  41.7 0.0 copy-done.2
  41.7 0.0 copy-done.9
  41.7 0.0 copy-done.10
  41.7 2.7 %last.1 = (f32[4,32,64,256]{3,2,1,0:T(8,128)}, f32[16,2048]{1,0:T(8,128)}) custom-call(f32[4,32,64,256]{3,2,1,0:T(8,128)} %get-tuple-element.18.state, f32[32,64,128]{2,1,0:T(8,128)S(1)} %get-tuple-element.19.kept, f32[128,128]{1,0:T(8,128)S(1)} %bitcast.9, f32[128,128]{1,0:T(8,128)S(1)} %copy-done.1, ...), custom_call_target="tpu_custom_call", output_to_operand_aliasing={{0}: (0, {})} | custom-call | bytes 9000000 | tf_op jit(solution)/shard_map/last/pallas_call | solution.py:554
  (11 shorter events, 0.0 us)
Async XLA Ops:
  0.6 41.0 %copy-start = (f32[16,2048]{1,0:T(8,128)S(1)}, f32[16,2048]{1,0:T(8,128)}, u32[]{:S(2)}) copy-start(f32[16,2048]{1,0:T(8,128)} %metal.1) | copy-start | bytes 393220
  0.6 41.0 %copy-start.3 = (f32[64,64]{1,0:T(8,128)S(1)}, f32[64,64]{1,0:T(8,128)}, u32[]{:S(2)}) copy-start(f32[64,64]{1,0:T(8,128)} %wall_inv.1) | copy-start | bytes 49156
  0.7 41.0 %copy-start.5 = (f32[2,1024]{1,0:T(2,128)S(1)}, f32[2,1024]{1,0:T(2,128)}, u32[]{:S(2)}) copy-start(f32[2,1024]{1,0:T(2,128)} %coef.1) | copy-start | bytes 24580
  0.7 41.0 %copy-start.6 = (f32[16,16]{1,0:T(8,128)S(1)}, f32[16,16]{1,0:T(8,128)}, u32[]{:S(2)}) copy-start(f32[16,16]{1,0:T(8,128)} %metal_inv.1) | copy-start | bytes 3076
  0.7 41.0 %copy-start.7 = (s32[1024,1]{0,1:T(1,128)S(1)}, s32[1024,1]{0,1:T(1,128)}, u32[]{:S(2)}) copy-start(s32[1024,1]{0,1:T(1,128)} %param.16) | copy-start | bytes 12292
  0.7 41.0 %copy-start.8 = (s32[1024]{0:T(1024)S(1)}, s32[1024]{0:T(1024)}, u32[]{:S(2)}) copy-start(s32[1024]{0:T(1024)} %param.17) | copy-start | bytes 12292
  11.0 30.7 %copy-start.1 = (f32[128,128]{1,0:T(8,128)S(1)}, f32[128,128]{1,0:T(8,128)}, u32[]{:S(2)}) copy-start(f32[128,128]{1,0:T(8,128)} %get-tuple-element.20.send) | copy-start | bytes 196612
  11.0 30.7 %copy-start.2 = (f32[16,2048]{1,0:T(8,128)S(1)}, f32[16,2048]{1,0:T(8,128)}, u32[]{:S(2)}) copy-start(f32[16,2048]{1,0:T(8,128)} %get-tuple-element.21.free) | copy-start | bytes 393220
  11.0 19.2 %collective-permute-start = (f32[4,64,256]{2,1,0:T(8,128)}, f32[4,64,256]{2,1,0:T(8,128)S(1)}, u32[]{:S(2)}, u32[]{:S(2)}) collective-permute-start(f32[4,64,256]{2,1,0:T(8,128)} %get-tuple-element.14), channel_id=1, source_target_pairs={{0,16},{16,32},{32,48},{48,64},{64,80},{80,96},{96,112},{112,0},{1... | collective-permute-start | bytes 786440 | tf_op jit(solution)/shard_map/ppermute | solution.py:534
  13.7 16.5 %collective-permute-start.1 = (f32[4,64,256]{2,1,0:T(8,128)}, f32[4,64,256]{2,1,0:T(8,128)S(1)}, u32[]{:S(2)}, u32[]{:S(2)}) collective-permute-start(f32[4,64,256]{2,1,0:T(8,128)} %get-tuple-element.15), channel_id=1, source_target_pairs={{16,0},{32,16},{48,32},{64,48},{80,64},{96,80},{112,96},{0,112},{1... | collective-permute-start | bytes 786440 | tf_op jit(solution)/shard_map/ppermute | solution.py:535
  13.7 16.4 %collective-permute-start.2 = (f32[4,32,256]{2,1,0:T(8,128)}, f32[4,32,256]{2,1,0:T(8,128)S(1)}, u32[]{:S(2)}, u32[]{:S(2)}) collective-permute-start(f32[4,32,256]{2,1,0:T(8,128)} %get-tuple-element.16), channel_id=1, source_target_pairs={{0,1},{1,2},{2,3},{3,4},{4,5},{5,6},{6,7},{7,8},{8,9},{9,10},{10,1... | collective-permute-start | bytes 393224 | tf_op jit(solution)/shard_map/ppermute | solution.py:536
  17.2 12.9 %collective-permute-start.3 = (f32[4,32,256]{2,1,0:T(8,128)}, f32[4,32,256]{2,1,0:T(8,128)S(1)}, u32[]{:S(2)}, u32[]{:S(2)}) collective-permute-start(f32[4,32,256]{2,1,0:T(8,128)} %get-tuple-element.17), channel_id=1, source_target_pairs={{1,0},{2,1},{3,2},{4,3},{5,4},{6,5},{7,6},{8,7},{9,8},{10,9},{11,1... | collective-permute-start | bytes 393224 | tf_op jit(solution)/shard_map/ppermute | solution.py:537
  18.5 23.1 %all-to-all-start = ((f32[128,1,128]{2,1,0:T(1,128)}), f32[128,1,128]{2,1,0:T(1,128)S(1)}, u32[]{:S(2)}, u32[]{:S(2)}) async-start(f32[128,1,128]{2,1,0:T(1,128)} %bitcast.8), calls=%async_computation | async-start | bytes 131072 | tf_op jit(solution)/shard_map/all_to_all | solution.py:529
  30.1 0.8 %copy-start.4 = (f32[64,128]{1,0:T(8,128)S(1)}, f32[64,128]{1,0:T(8,128)}, u32[]{:S(2)}) copy-start(f32[64,128]{1,0:T(8,128)} %get-tuple-element.13.walls) | copy-start | bytes 98308
  30.9 10.8 %copy-start.9 = (s32[1,1024]{1,0:T(1,128)S(1)}, s32[1,1024]{1,0:T(1,128)}, u32[]{:S(2)}) copy-start(s32[1,1024]{1,0:T(1,128)} %get-tuple-element.22.rank) | copy-start | bytes 12292
  30.9 10.8 %copy-start.10 = (f32[1,1024]{1,0:T(1,128)S(1)}, f32[1,1024]{1,0:T(1,128)}, u32[]{:S(2)}) copy-start(f32[1,1024]{1,0:T(1,128)} %get-tuple-element.23.top) | copy-start | bytes 12292
where the time goes:
time: 44.7 us; the launch traced here: 44.4 us
  Pallas kernels  23.6 us (53%)
  starting transfers between devices  19.1 us (43%)
  between operations  0.87 us (2%)
  local copies, waits for them, and re-layouts  0.79 us (2%)
    all_to_all x1, starting transfers between devices, local(): recv = lax.all_to_all(send, AXES, split_axis=0, concat_axis=0, tiled=True)  11.6 us
    pallas_call x1, Pallas kernels, local(): pl.pallas_call(stencil_kernel, name='stencil', in_specs=[spec(ANY), spec(...  10.7 us
    pallas_call x1, Pallas kernels, local(): pl.pallas_call(first_kernel, name='first', in_specs=[spec(HBM)] * 10, out...  10.3 us
    ppermute x1, starting transfers between devices, local(): prev_s = lax.ppermute(last_s, 'span', up_s)  3.53 us
    pallas_call x1, Pallas kernels, local(): pl.pallas_call(last_kernel, name='last', in_specs=[spec(ANY)] + [spec(VM)...  2.71 us
    ppermute x1, starting transfers between devices, local(): prev_p = lax.ppermute(last_p, 'pitch', up_p)  2.7 us
    ppermute x1, starting transfers between devices, local(): next_s = lax.ppermute(first_s, 'span', [(j, i) for i, j in up_s])  1.29 us
  transfers between devices with their start and end apart: 5, of which 0 were waited for; matrix products, arithmetic and copies ran while one was open for 0% of the time, Pallas kernels for 24%

commit v1 on v0

--- a/solution.py
+++ b/solution.py
@@ -25,6 +25,7 @@
 VMEM_WHOLE = 60 * 1024 * 1024
 FB = 256
 PAD = 8
+ROOM = 32
 
 
 def iota(shape, dim):
@@ -80,7 +81,7 @@
 def first_kernel(
     state, *args,
 ):
-    sources, (send, first_p, last_p, first_s, last_s, rank, top, free, walls) = args[:9], args[9:18]
+    sources, (send, give_pa, give_pb, give_sa, give_sb, rank, top, free, force_out) = args[:9], args[9:18]
     cur, lowb, temp, force, out_send, edge_p, edge_s, sems, *held = args[18:]
     col, low, owner, coef, cell, wall_inv, metal_inv, metal, conduct = held
     small = [
@@ -89,6 +90,7 @@
     ]
     for copy in small:
         copy.start()
+    odd_p, odd_s = lax.axis_index("pitch") & 1, lax.axis_index("span") & 1
     columns = state.reshape(4, COLS, GN)
     loads = []
     for i, c in enumerate((2, 0, 1, 3)):
@@ -103,8 +105,8 @@
     for copy in loads:
         copy.start()
     edges_in = [
-        pltpu.make_async_copy(state.at[:, 0], edge_p.at[0], sems.at[4]),
-        pltpu.make_async_copy(state.at[:, CP - 1], edge_p.at[1], sems.at[5]),
+        pltpu.make_async_copy(state.at[:, (1 - odd_p) * (CP - 1)], edge_p.at[0], sems.at[4]),
+        pltpu.make_async_copy(state.at[:, odd_p * (CP - 1)], edge_p.at[1], sems.at[5]),
     ]
     for copy in edges_in:
         copy.start()
@@ -152,8 +154,8 @@
     for copy in edges_in:
         copy.wait()
     edges_out = [
-        pltpu.make_async_copy(edge_p.at[0], first_p, sems.at[4]),
-        pltpu.make_async_copy(edge_p.at[1], last_p, sems.at[5]),
+        pltpu.make_async_copy(edge_p.at[0], give_pa, sems.at[4]),
+        pltpu.make_async_copy(edge_p.at[1], give_pb, sems.at[5]),
     ]
     for copy in edges_out:
         copy.start()
@@ -177,6 +179,9 @@
         return 0
 
     lax.fori_loop(0, FACES // 8, body, 0, unroll=8)
+
+    give = [pltpu.make_async_copy(force, force_out.at[0], sems.at[11])]
+    give[0].start()
 
     g = wall_inv[...]
     g_hi, g_lo = split2(g)
@@ -207,8 +212,8 @@
         total = total + dot_nt(cast(hot), cast(jnp.concatenate(pieces, axis=0)))
     total = total + pltpu.roll(total, 96, 1) + pltpu.roll(total, 64, 1)
     out_send[...] = jnp.where(lane < 32, own_half, jnp.where(lane < 64, total, 0.0))
-    give = [pltpu.make_async_copy(out_send, send, sems.at[6])]
-    give[0].start()
+    give.append(pltpu.make_async_copy(out_send, send, sems.at[6]))
+    give[1].start()
 
     for copy in loads[6:]:
         copy.wait()
@@ -216,15 +221,22 @@
         for h in range(2):
             lanes = slice(128 * h, 128 * h + 128)
             for p in range(0, CP, 8):
-                edge_s[0, c, p : p + 8, lanes] = halves[c][h][pl.ds(p * CS, 8, stride=CS), :]
-                edge_s[1, c, p : p + 8, lanes] = halves[c][h][
-                    pl.ds(p * CS + CS - 1, 8, stride=CS), :
-                ]
-    give.append(pltpu.make_async_copy(edge_s.at[0], first_s, sems.at[7]))
-    give.append(pltpu.make_async_copy(edge_s.at[1], last_s, sems.at[8]))
-    give[1].start()
-    give[2].start()
-
+                for k, row in enumerate(((1 - odd_s) * (CS - 1), odd_s * (CS - 1))):
+                    edge_s[k, c, p : p + 8, lanes] = halves[c][h][
+                        pl.ds(p * CS + row, 8, stride=CS), :
+                    ]
+    give.append(pltpu.make_async_copy(edge_s.at[0], give_sa, sems.at[7]))
+    give.append(pltpu.make_async_copy(edge_s.at[1], give_sb, sems.at[8]))
+    give[-1].start()
+    give[-2].start()
+    for copy in edges_out + give:
+        copy.wait()
+
+
+def drag(force, coef, cell, wall_inv, walls):
+    g_hi, g_lo = split2(wall_inv[...])
+    top_hi, top_lo = g_hi[0:1, :], g_lo[0:1, :]
+    none = jnp.zeros((1, WM), F32)
     blank = jnp.zeros((WM, WM), F32)
 
     def twice(part):
@@ -289,8 +301,6 @@
         total = total + dot_nt(cast(span_hot), cast(jnp.concatenate(pieces, axis=0)))
     walls[...] = jnp.zeros((CS, 128), F32)
     walls[:, 0:64] = -0.5 * (total[:, 0:64] + total[:, 64:128] + total[:, 128:192])
-    for copy in edges_out + give:
-        copy.wait()
 
 
 GROUP = 4
@@ -298,8 +308,15 @@
 ROWS = CS + 2 * HALO
 
 
-def stencil_kernel(state, walls, prev_p, next_p, prev_s, next_s, out, kept, cur, work, sems):
+def stencil_kernel(
+    state, force_in, coef, cell, wall_inv, got_pa, got_pb, got_sa, got_sb,
+    out, kept,
+    cur, work, force, walls, y_even, y_odd, sems,
+):
+    odd_p, odd_s = lax.axis_index("pitch") & 1, lax.axis_index("span") & 1
     inner = pl.ds(HALO, CS)
+    bring = pltpu.make_async_copy(force_in.at[0], force, sems.at[9])
+    bring.start()
     loads = []
     for c in range(4):
         for h in range(2):
@@ -309,24 +326,32 @@
                     state.at[c, :, :, lanes], cur.at[h, c, pl.ds(1, CP), inner, :], sems.at[c]
                 )
             )
-            if c == 0:
-                for plane, source in ((0, prev_p), (CP + 1, next_p)):
-                    loads.append(
-                        pltpu.make_async_copy(
-                            source.at[:, :, lanes], cur.at[h, :, plane, inner, :], sems.at[4]
-                        )
-                    )
-    for copy in loads:
+    edges = []
+    for h in range(2):
+        lanes = pl.ds(128 * h, 128)
+        for plane, source in (((1 - odd_p) * (CP + 1), got_pa), (odd_p * (CP + 1), got_pb)):
+            edges.append(
+                pltpu.make_async_copy(
+                    source.at[:, :, lanes], cur.at[h, :, plane, inner, :], sems.at[4]
+                )
+            )
+    for copy in loads[:2] + edges + loads[2:]:
         copy.start()
 
     flat = cur.reshape(2 * 4 * (CP + 2) * ROWS, 128)
+    below, above = HALO - 1, HALO + CS
+    row_a = above + odd_s * (below - above)
+    row_b = below + odd_s * (above - below)
     for h in range(2):
         lanes = slice(128 * h, 128 * h + 128)
         for c in range(4):
             for p in range(0, CP, 8):
                 start = ((h * 4 + c) * (CP + 2) + 1 + p) * ROWS
-                flat[pl.ds(start + HALO - 1, 8, stride=ROWS), :] = prev_s[c, p : p + 8, lanes]
-                flat[pl.ds(start + HALO + CS, 8, stride=ROWS), :] = next_s[c, p : p + 8, lanes]
+                flat[pl.ds(start + row_a, 8, stride=ROWS), :] = got_sa[c, p : p + 8, lanes]
+                flat[pl.ds(start + row_b, 8, stride=ROWS), :] = got_sb[c, p : p + 8, lanes]
+
+    bring.wait()
+    drag(force, coef, cell, wall_inv, walls)
 
     i, j = iota((GN, GN), 0), iota((GN, GN), 1)
     near = jnp.where(jnp.abs(i - j) == 1, 1.0, 0.0)
@@ -339,41 +364,52 @@
         lanes = pl.ds(128 * h, 128)
         return pltpu.make_async_copy(work.at[h, c], out.at[c, :, :, lanes], sems.at[5 + c])
 
-    for copy in loads[0:6]:
+    steps = CP // GROUP
+
+    def along(t, y):
+        c, p = t // steps, (t % steps) * GROUP
+        split = []
+        for q in range(GROUP):
+            a_hi, a_lo = split2(cur[0, c, p + 1 + q, HALO : HALO + CS, :])
+            b_hi, b_lo = split2(cur[1, c, p + 1 + q, HALO : HALO + CS, :])
+            split.append(jnp.concatenate([cast(x) for x in (a_hi, b_hi, a_lo, b_lo)], axis=1))
+        y[...] = dot_nn(jnp.concatenate(split, axis=0), matrix)
+
+    def finish(c, n, y):
+        p = n * GROUP
+        for q in range(GROUP):
+            for h in range(2):
+                up = cur[h, c, p + 1 + q, HALO + 1 : HALO + CS + 1, :]
+                dn = cur[h, c, p + 1 + q, HALO - 1 : HALO + CS - 1, :]
+                after = cur[h, c, p + 2 + q, HALO : HALO + CS, :]
+                prior = cur[h, c, p + q, HALO : HALO + CS, :]
+                mid = y[CS * q : CS * (q + 1), 128 * h : 128 * (h + 1)]
+                value = 0.1 * (mid + (up + dn)) + (0.25 * prior - 0.05 * after)
+                if c < 2 and h == 0:
+                    wall = pltpu.roll(walls[...], 128 - (c * CP + p + q), 1)
+                    value = value + jnp.where(first_lane, wall, 0.0)
+                if c == 2 and h == 0:
+                    kept[p + q, :, :] = value
+                else:
+                    work[h, c, p + q, :, :] = value
+
+    for copy in loads[:2] + edges:
         copy.wait()
+    along(0, y_even)
     for c in range(4):
-        if c > 0:
-            loads[4 + 2 * c].wait()
-            loads[5 + 2 * c].wait()
+        if c < 3:
+            for copy in loads[2 * c + 2 : 2 * c + 4]:
+                copy.wait()
 
         def body(n, _):
-            p = n * GROUP
-            split = []
-            for q in range(GROUP):
-                a = cur[0, c, p + 1 + q, HALO : HALO + CS, :]
-                b = cur[1, c, p + 1 + q, HALO : HALO + CS, :]
-                a_hi, a_lo = split2(a)
-                b_hi, b_lo = split2(b)
-                split.append(jnp.concatenate([cast(x) for x in (a_hi, b_hi, a_lo, b_lo)], axis=1))
-            y = dot_nn(jnp.concatenate(split, axis=0), matrix)
-            for q in range(GROUP):
-                for h in range(2):
-                    up = cur[h, c, p + 1 + q, HALO + 1 : HALO + CS + 1, :]
-                    dn = cur[h, c, p + 1 + q, HALO - 1 : HALO + CS - 1, :]
-                    after = cur[h, c, p + 2 + q, HALO : HALO + CS, :]
-                    prior = cur[h, c, p + q, HALO : HALO + CS, :]
-                    mid = y[CS * q : CS * (q + 1), 128 * h : 128 * (h + 1)]
-                    value = 0.1 * (mid + (up + dn)) + (0.25 * prior - 0.05 * after)
-                    if c < 2 and h == 0:
-                        wall = pltpu.roll(walls[...], 128 - (c * CP + p + q), 1)
-                        value = value + jnp.where(first_lane, wall, 0.0)
-                    if c == 2 and h == 0:
-                        kept[p + q, :, :] = value
-                    else:
-                        work[h, c, p + q, :, :] = value
+            t = c * steps + 2 * n
+            along(t + 1, y_odd)
+            finish(c, 2 * n, y_even)
+            along(jnp.minimum(t + 2, 4 * steps - 1), y_even)
+            finish(c, 2 * n + 1, y_odd)
             return 0
 
-        lax.fori_loop(0, CP // GROUP, body, 0)
+        lax.fori_loop(0, steps // 2, body, 0)
         for h in range(2):
             if c != 2 or h == 1:
                 put(c, h).start()
@@ -385,8 +421,8 @@
 
 def last_kernel(
     state, kept, recv, send, free, metal, owner, rank, top, coef, cell, wall_inv, metal_inv,
-    out, metal_out,
-    sems,
+    out, metal_give,
+    metal_out, sems,
 ):
     corner_f = 0.5 * wall_inv[0:1, 0:1]
     corner_m = 0.5 * metal_inv[0:1, 0:1]
@@ -442,6 +478,9 @@
         metal_out[:, cols] = jnp.where(
             used_row > 0.5, free[:, cols] + gain * tw_row, metal[:, cols]
         )
+    give = pltpu.make_async_copy(metal_out, metal_give, sems.at[1])
+    give.start()
+    give.wait()
     copy.wait()
 
 
@@ -484,11 +523,11 @@
     cell = face_cell.reshape(1, FACES)
     low = sample_low.reshape(1, FACES)
     conduct = metal_conduct.reshape(16, 128)
-    send, first_p, last_p, first_s, last_s, rank, top, free, walls = pl.pallas_call(
+    send, give_pa, give_pb, give_sa, give_sb, rank, top, free, force = pl.pallas_call(
         first_kernel,
         name="first",
         in_specs=[spec(HBM)] * 10,
-        out_specs=[spec(ANY)] * 5 + [spec(VM)] * 4,
+        out_specs=[spec(HBM)] * 5 + [spec(VM)] * 3 + [spec(HBM)],
         out_shape=[
             shape((DEV, 128)),
             shape((4, CS, GN)),
@@ -498,7 +537,7 @@
             shape((1, FACES), I32),
             shape((1, FACES)),
             shape((MP, SLOT_DEV)),
-            shape((CS, 128)),
+            shape((ROOM, FACES, 128)),
         ],
         scratch_shapes=[
             pltpu.VMEM((8, COLS + PAD, 128), F32),
@@ -508,7 +547,7 @@
             pltpu.VMEM((DEV, 128), F32),
             pltpu.VMEM((2, 4, CS, GN), F32),
             pltpu.VMEM((2, 4, CP, GN), F32),
-            pltpu.SemaphoreType.DMA((11,)),
+            pltpu.SemaphoreType.DMA((12,)),
             pltpu.SMEM((FACES,), I32),
             pltpu.VMEM((1, FACES), I32),
             pltpu.VMEM((1, FACES), I32),
@@ -529,36 +568,42 @@
     recv = lax.all_to_all(send, AXES, split_axis=0, concat_axis=0, tiled=True)
 
     n_pitch, n_span = lax.axis_size("pitch"), lax.axis_size("span")
-    up_p = [(i, (i + 1) % n_pitch) for i in range(n_pitch)]
-    up_s = [(i, i + 1) for i in range(n_span - 1)]
-    prev_p = lax.ppermute(last_p, "pitch", up_p)
-    next_p = lax.ppermute(first_p, "pitch", [(j, i) for i, j in up_p])
-    prev_s = lax.ppermute(last_s, "span", up_s)
-    next_s = lax.ppermute(first_s, "span", [(j, i) for i, j in up_s])
+    within_p = [(i, i ^ 1) for i in range(n_pitch)]
+    across_p = [(i, (i + (1 if i & 1 else -1)) % n_pitch) for i in range(n_pitch)]
+    within_s = [(i, i ^ 1) for i in range(n_span)]
+    across_s = [(i, i + (1 if i & 1 else -1)) for i in range(1, n_span - 1)]
+    got_pa = lax.ppermute(give_pa, "pitch", within_p)
+    got_pb = lax.ppermute(give_pb, "pitch", across_p)
+    got_sa = lax.ppermute(give_sa, "span", within_s)
+    got_sb = lax.ppermute(give_sb, "span", across_s)
 
     new_state, kept = pl.pallas_call(
         stencil_kernel,
         name="stencil",
-        in_specs=[spec(ANY), spec(VM), spec(ANY), spec(ANY), spec(VM), spec(VM)],
+        in_specs=[spec(ANY), spec(ANY)] + [spec(VM)] * 3 + [spec(ANY)] * 2 + [spec(VM)] * 2,
         out_specs=[spec(ANY), spec(VM)],
         out_shape=[shape((4, CP, CS, GN)), shape((CP, CS, 128))],
         scratch_shapes=[
             pltpu.VMEM((2, 4, CP + 2, ROWS, 128), F32),
             pltpu.VMEM((2, 4, CP, CS, 128), F32),
-            pltpu.SemaphoreType.DMA((9,)),
+            pltpu.VMEM((FACES, 128), F32),
+            pltpu.VMEM((CS, 128), F32),
+            pltpu.VMEM((GROUP * CS, GN), F32),
+            pltpu.VMEM((GROUP * CS, GN), F32),
+            pltpu.SemaphoreType.DMA((10,)),
         ],
         compiler_params=params(),
-        cost_estimate=cost(8),
-    )(flow_state, walls, prev_p, next_p, prev_s, next_s)
+        cost_estimate=cost(10),
+    )(flow_state, force, face_coef, cell, wall_inverse, got_pa, got_pb, got_sa, got_sb)
 
     new_state, metal_out = pl.pallas_call(
         last_kernel,
         name="last",
         in_specs=[spec(ANY)] + [spec(VM)] * 12,
-        out_specs=[spec(ANY), spec(VM)],
+        out_specs=[spec(ANY), spec(HBM)],
         out_shape=[shape((4, CP, CS, GN)), shape((MP, SLOT_DEV))],
         input_output_aliases={0: 0},
-        scratch_shapes=[pltpu.SemaphoreType.DMA((1,))],
+        scratch_shapes=[pltpu.VMEM((MP, SLOT_DEV), F32), pltpu.SemaphoreType.DMA((2,))],
         compiler_params=params(),
         cost_estimate=cost(3),
     )(

time: 44.7 us -> 37.5 us (0.84)
  starting transfers between devices: 19.1 us -> 15.9 us
  Pallas kernels: 23.6 us -> 20.6 us
  local copies, waits for them, and re-layouts: 0.79 us -> 0.05 us
    ppermute x4, starting transfers between devices: 7.53 us -> 5.16 us  [the longest x1 1.64 us: local(): got_sa = lax.ppermute(give_sa, 'span', within_s)]
    pallas_call x1, Pallas kernels: 10.3 us -> 8.78 us  [local(): pl.pallas_call(first_kernel, name='first', in_specs=[spec(HBM)] * 10, out...]
    pallas_call x1, Pallas kernels: 10.7 us -> 9.69 us  [local(): pl.pallas_call(stencil_kernel, name='stencil', in_specs=[spec(ANY), spec(...]
    all_to_all x1, starting transfers between devices: 11.6 us -> 10.8 us  [local(): recv = lax.all_to_all(send, AXES, split_axis=0, concat_axis=0, tiled=True)]
    unnamed x22 -> x20, local copies, waits for them, and re-layouts: 0.79 us -> 0.05 us
    pallas_call x1, Pallas kernels: 2.71 us -> 2.1 us  [local(): pl.pallas_call(last_kernel, name='last', in_specs=[spec(ANY)] + [spec(VM)...]
  transfers between devices with their start and end apart: 5 -> 5, of which waited for: 0 -> 0; matrix products, arithmetic and copies ran while one was open for 0% -> 0% of each run, Pallas kernels for 24% -> 26%
where the time goes in v1:
time: 37.5 us; the launch traced here: 37.4 us
  Pallas kernels  20.6 us (55%)
  starting transfers between devices  15.9 us (42%)
  between operations  0.86 us (2%)
    all_to_all x1, starting transfers between devices, local(): recv = lax.all_to_all(send, AXES, split_axis=0, concat_axis=0, tiled=True)  10.8 us
    pallas_call x1, Pallas kernels, local(): pl.pallas_call(stencil_kernel, name='stencil', in_specs=[spec(ANY), spec(...  9.69 us
    pallas_call x1, Pallas kernels, local(): pl.pallas_call(first_kernel, name='first', in_specs=[spec(HBM)] * 10, out...  8.78 us
    pallas_call x1, Pallas kernels, local(): pl.pallas_call(last_kernel, name='last', in_specs=[spec(ANY)] + [spec(VM)...  2.1 us
    ppermute x1, starting transfers between devices, local(): got_sa = lax.ppermute(give_sa, 'span', within_s)  1.64 us
    ppermute x1, starting transfers between devices, local(): got_pa = lax.ppermute(give_pa, 'pitch', within_p)  1.51 us
    ppermute x1, starting transfers between devices, local(): got_pb = lax.ppermute(give_pb, 'pitch', across_p)  1.35 us
  transfers between devices with their start and end apart: 5, of which 0 were waited for; matrix products, arithmetic and copies ran while one was open for 0% of the time, Pallas kernels for 26%

profile of v1, /device:TPU:1, one launch (start us, length us, event | category | flops | bytes accessed | tf_op | source)
XLA Modules:
  0.0 37.4 jit_solution(11200726513998404240)
XLA Ops:
  0.7 8.8 %first.1 = (f32[128,128]{1,0:T(8,128)}, f32[4,64,256]{2,1,0:T(8,128)}, f32[4,64,256]{2,1,0:T(8,128)}, f32[4,32,256]{2,1,0:T(8,128)}, f32[4,32,256]{2,1,0:T(8,128...) custom-call(f32[4,32,64,256]{3,2,1,0:T(8,128)} %state.3, ...), custom_call_target="tpu_custom_call" | custom-call | bytes 21000000 | tf_op jit(solution)/shard_map/first/pallas_call | solution.py:526
  9.5 1.5 %collective-permute-start = (f32[4,64,256]{2,1,0:T(8,128)}, f32[4,64,256]{2,1,0:T(8,128)S(1)}, u32[]{:S(2)}, u32[]{:S(2)}) collective-permute-start(f32[4,64,256]{2,1,0:T(8,128)} %get-tuple-element.14), channel_id=1, source_target_pairs={{0,16},{16,0},{32,48},{48,32},{64,80},{80,64},{96,112},{112,96},{1... | collective-permute-start | bytes 786440 | tf_op jit(solution)/shard_map/ppermute | solution.py:575
  11.0 1.4 %collective-permute-start.1 = (f32[4,64,256]{2,1,0:T(8,128)}, f32[4,64,256]{2,1,0:T(8,128)S(1)}, u32[]{:S(2)}, u32[]{:S(2)}) collective-permute-start(f32[4,64,256]{2,1,0:T(8,128)} %get-tuple-element.15), channel_id=1, source_target_pairs={{0,112},{16,32},{32,16},{48,64},{64,48},{80,96},{96,80},{112,0},{1... | collective-permute-start | bytes 786440 | tf_op jit(solution)/shard_map/ppermute | solution.py:576
  12.3 1.6 %collective-permute-start.2 = (f32[4,32,256]{2,1,0:T(8,128)}, f32[4,32,256]{2,1,0:T(8,128)S(1)}, u32[]{:S(2)}, u32[]{:S(2)}) collective-permute-start(f32[4,32,256]{2,1,0:T(8,128)} %get-tuple-element.16), channel_id=1, source_target_pairs={{0,1},{1,0},{2,3},{3,2},{4,5},{5,4},{6,7},{7,6},{8,9},{9,8},{10,11... | collective-permute-start | bytes 393224 | tf_op jit(solution)/shard_map/ppermute | solution.py:577
  14.0 0.7 %collective-permute-start.3 = (f32[4,32,256]{2,1,0:T(8,128)}, f32[4,32,256]{2,1,0:T(8,128)S(1)}, u32[]{:S(2)}, u32[]{:S(2)}) collective-permute-start(f32[4,32,256]{2,1,0:T(8,128)} %get-tuple-element.17), channel_id=1, source_target_pairs={{1,2},{2,1},{3,4},{4,3},{5,6},{6,5},{7,8},{8,7},{9,10},{10,9},{11,... | collective-permute-start | bytes 393224 | tf_op jit(solution)/shard_map/ppermute | solution.py:578
  14.6 10.8 %all-to-all-start = ((f32[128,1,128]{2,1,0:T(1,128)}), f32[128,1,128]{2,1,0:T(1,128)S(1)}, u32[]{:S(2)}, u32[]{:S(2)}) async-start(f32[128,1,128]{2,1,0:T(1,128)} %bitcast.8), calls=%async_computation | async-start | bytes 131072 | tf_op jit(solution)/shard_map/all_to_all | solution.py:568
  25.4 0.0 collective-permute-done.2.got_sa
  25.4 0.0 collective-permute-done.3.got_sb
  25.4 0.0 collective-permute-done.got_pa
  25.4 0.0 collective-permute-done.1.got_pb
  25.4 0.0 copy-done.5
  25.4 0.0 copy-done.1
  25.4 0.0 copy-done.4
  25.5 0.0 copy-start
  25.5 0.0 copy-start.6
  25.5 0.0 copy-start.7
  25.5 9.7 %stencil.1 = (f32[4,32,64,256]{3,2,1,0:T(8,128)}, f32[32,64,128]{2,1,0:T(8,128)S(1)}) custom-call(f32[4,32,64,256]{3,2,1,0:T(8,128)} %state.3, f32[32,1024,128]{2,1,0:T(8,128)} %get-tuple-element.13.force_in, f32[2,1024]{1,0:T(2,128)S(1)} %copy-done.4, s32[1,1024]{1,0:T(1,128)S(1)} %bitcast.11, f32[64,64]{1,0:T(8,128)S(1)} %copy-done.1, ...), custom_call_target="tpu_custom_call" | custom-call | bytes 30000000 | tf_op jit(solution)/shard_map/stencil/pallas_call | solution.py:580
  35.2 0.0 all-to-all-done
  35.2 0.0 copy-done
  35.2 0.0 copy-done.2
  35.3 0.0 copy-done.3
  35.3 0.0 copy-done.6
  35.3 0.0 copy-done.7
  35.3 2.1 %last.1 = (f32[4,32,64,256]{3,2,1,0:T(8,128)}, f32[16,2048]{1,0:T(8,128)}) custom-call(f32[4,32,64,256]{3,2,1,0:T(8,128)} %get-tuple-element.18.state, f32[32,64,128]{2,1,0:T(8,128)S(1)} %get-tuple-element.19.kept, f32[128,128]{1,0:T(8,128)S(1)} %bitcast.9, f32[128,128]{1,0:T(8,128)S(1)} %copy-done.2, ...), custom_call_target="tpu_custom_call", output_to_operand_aliasing={{0}: (0, {})} | custom-call | bytes 9000000 | tf_op jit(solution)/shard_map/last/pallas_call | solution.py:599
  (9 shorter events, 0.0 us)
Async XLA Ops:
  0.6 24.8 %copy-start.5 = (s32[1024]{0:T(1024)S(1)}, s32[1024]{0:T(1024)}, u32[]{:S(2)}) copy-start(s32[1024]{0:T(1024)} %param.17) | copy-start | bytes 12292
  0.6 24.8 %copy-start.1 = (f32[64,64]{1,0:T(8,128)S(1)}, f32[64,64]{1,0:T(8,128)}, u32[]{:S(2)}) copy-start(f32[64,64]{1,0:T(8,128)} %wall_inv.3) | copy-start | bytes 49156
  0.7 24.8 %copy-start.4 = (f32[2,1024]{1,0:T(2,128)S(1)}, f32[2,1024]{1,0:T(2,128)}, u32[]{:S(2)}) copy-start(f32[2,1024]{1,0:T(2,128)} %coef.3) | copy-start | bytes 24580
  9.5 16.0 %collective-permute-start = (f32[4,64,256]{2,1,0:T(8,128)}, f32[4,64,256]{2,1,0:T(8,128)S(1)}, u32[]{:S(2)}, u32[]{:S(2)}) collective-permute-start(f32[4,64,256]{2,1,0:T(8,128)} %get-tuple-element.14), channel_id=1, source_target_pairs={{0,16},{16,0},{32,48},{48,32},{64,80},{80,64},{96,112},{112,96},{1... | collective-permute-start | bytes 786440 | tf_op jit(solution)/shard_map/ppermute | solution.py:575
  11.0 14.5 %collective-permute-start.1 = (f32[4,64,256]{2,1,0:T(8,128)}, f32[4,64,256]{2,1,0:T(8,128)S(1)}, u32[]{:S(2)}, u32[]{:S(2)}) collective-permute-start(f32[4,64,256]{2,1,0:T(8,128)} %get-tuple-element.15), channel_id=1, source_target_pairs={{0,112},{16,32},{32,16},{48,64},{64,48},{80,96},{96,80},{112,0},{1... | collective-permute-start | bytes 786440 | tf_op jit(solution)/shard_map/ppermute | solution.py:576
  12.3 13.1 %collective-permute-start.2 = (f32[4,32,256]{2,1,0:T(8,128)}, f32[4,32,256]{2,1,0:T(8,128)S(1)}, u32[]{:S(2)}, u32[]{:S(2)}) collective-permute-start(f32[4,32,256]{2,1,0:T(8,128)} %get-tuple-element.16), channel_id=1, source_target_pairs={{0,1},{1,0},{2,3},{3,2},{4,5},{5,4},{6,7},{7,6},{8,9},{9,8},{10,11... | collective-permute-start | bytes 393224 | tf_op jit(solution)/shard_map/ppermute | solution.py:577
  14.0 11.4 %collective-permute-start.3 = (f32[4,32,256]{2,1,0:T(8,128)}, f32[4,32,256]{2,1,0:T(8,128)S(1)}, u32[]{:S(2)}, u32[]{:S(2)}) collective-permute-start(f32[4,32,256]{2,1,0:T(8,128)} %get-tuple-element.17), channel_id=1, source_target_pairs={{1,2},{2,1},{3,4},{4,3},{5,6},{6,5},{7,8},{8,7},{9,10},{10,9},{11,... | collective-permute-start | bytes 393224 | tf_op jit(solution)/shard_map/ppermute | solution.py:578
  14.6 20.6 %all-to-all-start = ((f32[128,1,128]{2,1,0:T(1,128)}), f32[128,1,128]{2,1,0:T(1,128)S(1)}, u32[]{:S(2)}, u32[]{:S(2)}) async-start(f32[128,1,128]{2,1,0:T(1,128)} %bitcast.8), calls=%async_computation | async-start | bytes 131072 | tf_op jit(solution)/shard_map/all_to_all | solution.py:568
  25.5 9.8 %copy-start = (f32[16,2048]{1,0:T(8,128)S(1)}, f32[16,2048]{1,0:T(8,128)}, u32[]{:S(2)}) copy-start(f32[16,2048]{1,0:T(8,128)} %metal.1) | copy-start | bytes 393220
  25.5 9.8 %copy-start.2 = (f32[128,128]{1,0:T(8,128)S(1)}, f32[128,128]{1,0:T(8,128)}, u32[]{:S(2)}) copy-start(f32[128,128]{1,0:T(8,128)} %get-tuple-element.20.send) | copy-start | bytes 196612
  25.5 9.8 %copy-start.3 = (f32[16,2048]{1,0:T(8,128)S(1)}, f32[16,2048]{1,0:T(8,128)}, u32[]{:S(2)}) copy-start(f32[16,2048]{1,0:T(8,128)} %get-tuple-element.21.free) | copy-start | bytes 393220
  25.5 9.8 %copy-start.6 = (f32[16,16]{1,0:T(8,128)S(1)}, f32[16,16]{1,0:T(8,128)}, u32[]{:S(2)}) copy-start(f32[16,16]{1,0:T(8,128)} %metal_inv.1) | copy-start | bytes 3076
  25.5 9.8 %copy-start.7 = (s32[1024,1]{0,1:T(1,128)S(1)}, s32[1024,1]{0,1:T(1,128)}, u32[]{:S(2)}) copy-start(s32[1024,1]{0,1:T(1,128)} %param.16) | copy-start | bytes 12292
  25.5 9.8 %copy-start.8 = (s32[1,1024]{1,0:T(1,128)S(1)}, s32[1,1024]{1,0:T(1,128)}, u32[]{:S(2)}) copy-start(s32[1,1024]{1,0:T(1,128)} %get-tuple-element.22.rank) | copy-start | bytes 12292
  25.5 9.8 %copy-start.9 = (f32[1,1024]{1,0:T(1,128)S(1)}, f32[1,1024]{1,0:T(1,128)}, u32[]{:S(2)}) copy-start(f32[1,1024]{1,0:T(1,128)} %get-tuple-element.23.top) | copy-start | bytes 12292

commit v2 on v1

--- a/solution.py
+++ b/solution.py
@@ -102,14 +102,12 @@
                     sems.at[i],
                 )
             )
-    for copy in loads:
+    for copy in loads[:6]:
         copy.start()
     edges_in = [
         pltpu.make_async_copy(state.at[:, (1 - odd_p) * (CP - 1)], edge_p.at[0], sems.at[4]),
         pltpu.make_async_copy(state.at[:, odd_p * (CP - 1)], edge_p.at[1], sems.at[5]),
     ]
-    for copy in edges_in:
-        copy.start()
 
     for copy in small[1:]:
         copy.wait()
@@ -151,17 +149,11 @@
         carry = carry + jnp.sum(hot, axis=1, keepdims=True)
         rank[:, cols] = jnp.sum(hot * prior, axis=0, keepdims=True).astype(I32)
 
-    for copy in edges_in:
+    small[0].wait()
+    for copy in loads[:6]:
         copy.wait()
-    edges_out = [
-        pltpu.make_async_copy(edge_p.at[0], give_pa, sems.at[4]),
-        pltpu.make_async_copy(edge_p.at[1], give_pb, sems.at[5]),
-    ]
-    for copy in edges_out:
+    for copy in loads[6:] + edges_in:
         copy.start()
-    small[0].wait()
-    for copy in loads[0:6]:
-        copy.wait()
     halves = [[cur.at[2 * c + h] for h in range(2)] for c in range(4)]
     lane8 = iota((8, 128), 1)
     left = lane8 < WM
@@ -215,8 +207,14 @@
     give.append(pltpu.make_async_copy(out_send, send, sems.at[6]))
     give[1].start()
 
-    for copy in loads[6:]:
+    for copy in loads[6:] + edges_in:
         copy.wait()
+    edges_out = [
+        pltpu.make_async_copy(edge_p.at[0], give_pa, sems.at[4]),
+        pltpu.make_async_copy(edge_p.at[1], give_pb, sems.at[5]),
+    ]
+    for copy in edges_out:
+        copy.start()
     for c in range(4):
         for h in range(2):
             lanes = slice(128 * h, 128 * h + 128)
@@ -356,24 +354,27 @@
     i, j = iota((GN, GN), 0), iota((GN, GN), 1)
     near = jnp.where(jnp.abs(i - j) == 1, 1.0, 0.0)
     same = jnp.where((i == 0) | (i == GN - 1), 5.0, 4.0)
-    matrix = jnp.where(i == j, same, near)
-    matrix = cast(jnp.concatenate([matrix, matrix], axis=0))
+    matrix = cast(jnp.where(i == j, same, near))
     first_lane = iota((CS, 128), 1) == 0
 
-    def put(c, h):
+    def put(c, h, planes):
         lanes = pl.ds(128 * h, 128)
-        return pltpu.make_async_copy(work.at[h, c], out.at[c, :, :, lanes], sems.at[5 + c])
+        return pltpu.make_async_copy(
+            work.at[h, c, planes], out.at[c, planes, :, lanes], sems.at[5 + c]
+        )
 
     steps = CP // GROUP
 
     def along(t, y):
         c, p = t // steps, (t % steps) * GROUP
-        split = []
+        hi, lo = [], []
         for q in range(GROUP):
             a_hi, a_lo = split2(cur[0, c, p + 1 + q, HALO : HALO + CS, :])
             b_hi, b_lo = split2(cur[1, c, p + 1 + q, HALO : HALO + CS, :])
-            split.append(jnp.concatenate([cast(x) for x in (a_hi, b_hi, a_lo, b_lo)], axis=1))
-        y[...] = dot_nn(jnp.concatenate(split, axis=0), matrix)
+            hi.append(jnp.concatenate([cast(a_hi), cast(b_hi)], axis=1))
+            lo.append(jnp.concatenate([cast(a_lo), cast(b_lo)], axis=1))
+        hi, lo = jnp.concatenate(hi, axis=0), jnp.concatenate(lo, axis=0)
+        y[...] = dot_nn(hi, matrix) + dot_nn(lo, matrix)
 
     def finish(c, n, y):
         p = n * GROUP
@@ -407,16 +408,20 @@
             finish(c, 2 * n, y_even)
             along(jnp.minimum(t + 2, 4 * steps - 1), y_even)
             finish(c, 2 * n + 1, y_odd)
+            if c == 3:
+                for h in range(2):
+                    put(c, h, pl.ds(2 * n * GROUP, 2 * GROUP)).start()
             return 0
 
         lax.fori_loop(0, steps // 2, body, 0)
-        for h in range(2):
-            if c != 2 or h == 1:
-                put(c, h).start()
+        if c < 3:
+            for h in range(2):
+                if c != 2 or h == 1:
+                    put(c, h, pl.ds(0, CP)).start()
     for c in range(4):
         for h in range(2):
             if c != 2 or h == 1:
-                put(c, h).wait()
+                put(c, h, pl.ds(0, CP)).wait()
 
 
 def last_kernel(
@@ -448,11 +453,18 @@
     wall = -0.5 * (total[:, 0:32] + total[:, 32:64] + total[:, 64:96])
     wall = jnp.concatenate([wall, jnp.zeros((CS, 96), F32)], axis=1)
     first_lane = iota((CS, 128), 1) == 0
+    copies = []
     for p in range(CP):
         column = wall if p == 0 else pltpu.roll(wall, 128 - p, 1)
         kept[p] = kept[p] + jnp.where(first_lane, column, 0.0)
-    copy = pltpu.make_async_copy(kept, out.at[2, :, :, pl.ds(0, 128)], sems.at[0])
-    copy.start()
+        if p % 16 == 15:
+            planes = pl.ds(p - 15, 16)
+            copies.append(
+                pltpu.make_async_copy(
+                    kept.at[planes], out.at[2, planes, :, pl.ds(0, 128)], sems.at[len(copies)]
+                )
+            )
+            copies[-1].start()
 
     own = send[...]
     lane = iota((DEV, 128), 1)
@@ -478,10 +490,10 @@
         metal_out[:, cols] = jnp.where(
             used_row > 0.5, free[:, cols] + gain * tw_row, metal[:, cols]
         )
-    give = pltpu.make_async_copy(metal_out, metal_give, sems.at[1])
-    give.start()
-    give.wait()
-    copy.wait()
+    copies.append(pltpu.make_async_copy(metal_out, metal_give, sems.at[2]))
+    copies[-1].start()
+    for copy in copies:
+        copy.wait()
 
 
 def spec(space):
@@ -603,7 +615,7 @@
         out_specs=[spec(ANY), spec(HBM)],
         out_shape=[shape((4, CP, CS, GN)), shape((MP, SLOT_DEV))],
         input_output_aliases={0: 0},
-        scratch_shapes=[pltpu.VMEM((MP, SLOT_DEV), F32), pltpu.SemaphoreType.DMA((2,))],
+        scratch_shapes=[pltpu.VMEM((MP, SLOT_DEV), F32), pltpu.SemaphoreType.DMA((3,))],
         compiler_params=params(),
         cost_estimate=cost(3),
     )(

time: 37.5 us -> 36.5 us (0.973)
  Pallas kernels: 20.6 us -> 19.3 us
    pallas_call x1, Pallas kernels: 8.78 us -> 8.11 us  [local(): pl.pallas_call(first_kernel, name='first', in_specs=[spec(HBM)] * 10, out...]
    pallas_call x1, Pallas kernels: 9.69 us -> 9.03 us  [local(): pl.pallas_call(stencil_kernel, name='stencil', in_specs=[spec(ANY), spec(...]
  transfers between devices with their start and end apart: 5 -> 5, of which waited for: 0 -> 1; matrix products, arithmetic and copies ran while one was open for 0% -> 0% of each run, Pallas kernels for 26% -> 25%
where the time goes in v2:
time: 36.5 us; the launch traced here: 36.4 us
  Pallas kernels  19.3 us (53%)
  starting transfers between devices  15.9 us (44%)
  between operations  0.84 us (2%)
    all_to_all x1, starting transfers between devices, local(): recv = lax.all_to_all(send, AXES, split_axis=0, concat_axis=0, tiled=True)  10.8 us
    pallas_call x1, Pallas kernels, local(): pl.pallas_call(stencil_kernel, name='stencil', in_specs=[spec(ANY), spec(...  9.03 us
    pallas_call x1, Pallas kernels, local(): pl.pallas_call(first_kernel, name='first', in_specs=[spec(HBM)] * 10, out...  8.11 us
    pallas_call x1, Pallas kernels, local(): pl.pallas_call(last_kernel, name='last', in_specs=[spec(ANY)] + [spec(VM)...  2.11 us
    ppermute x1, starting transfers between devices, local(): got_sa = lax.ppermute(give_sa, 'span', within_s)  1.64 us
    ppermute x1, starting transfers between devices, local(): got_pa = lax.ppermute(give_pa, 'pitch', within_p)  1.51 us
    ppermute x1, starting transfers between devices, local(): got_pb = lax.ppermute(give_pb, 'pitch', across_p)  1.34 us
  transfers between devices with their start and end apart: 5, of which 1 were waited for; matrix products, arithmetic and copies ran while one was open for 0% of the time, Pallas kernels for 25%

profile of v2, /device:TPU:1, one launch (start us, length us, event | category | flops | bytes accessed | tf_op | source)
XLA Modules:
  0.0 36.4 jit_solution(4218700978382809111)
XLA Ops:
  0.6 0.0 copy-start.5
  0.6 0.0 copy-start.1
  0.7 0.0 copy-start.4
  0.7 8.1 %first.1 = (f32[128,128]{1,0:T(8,128)}, f32[4,64,256]{2,1,0:T(8,128)}, f32[4,64,256]{2,1,0:T(8,128)}, f32[4,32,256]{2,1,0:T(8,128)}, f32[4,32,256]{2,1,0:T(8,128...) custom-call(f32[4,32,64,256]{3,2,1,0:T(8,128)} %state.3, ...), custom_call_target="tpu_custom_call" | custom-call | bytes 21000000 | tf_op jit(solution)/shard_map/first/pallas_call | solution.py:538
  8.8 1.5 %collective-permute-start = (f32[4,64,256]{2,1,0:T(8,128)}, f32[4,64,256]{2,1,0:T(8,128)S(1)}, u32[]{:S(2)}, u32[]{:S(2)}) collective-permute-start(f32[4,64,256]{2,1,0:T(8,128)} %get-tuple-element.14), channel_id=1, source_target_pairs={{0,16},{16,0},{32,48},{48,32},{64,80},{80,64},{96,112},{112,96},{1... | collective-permute-start | bytes 786440 | tf_op jit(solution)/shard_map/ppermute | solution.py:587
  10.3 1.3 %collective-permute-start.1 = (f32[4,64,256]{2,1,0:T(8,128)}, f32[4,64,256]{2,1,0:T(8,128)S(1)}, u32[]{:S(2)}, u32[]{:S(2)}) collective-permute-start(f32[4,64,256]{2,1,0:T(8,128)} %get-tuple-element.15), channel_id=1, source_target_pairs={{0,112},{16,32},{32,16},{48,64},{64,48},{80,96},{96,80},{112,0},{1... | collective-permute-start | bytes 786440 | tf_op jit(solution)/shard_map/ppermute | solution.py:588
  11.6 1.6 %collective-permute-start.2 = (f32[4,32,256]{2,1,0:T(8,128)}, f32[4,32,256]{2,1,0:T(8,128)S(1)}, u32[]{:S(2)}, u32[]{:S(2)}) collective-permute-start(f32[4,32,256]{2,1,0:T(8,128)} %get-tuple-element.16), channel_id=1, source_target_pairs={{0,1},{1,0},{2,3},{3,2},{4,5},{5,4},{6,7},{7,6},{8,9},{9,8},{10,11... | collective-permute-start | bytes 393224 | tf_op jit(solution)/shard_map/ppermute | solution.py:589
  13.3 0.7 %collective-permute-start.3 = (f32[4,32,256]{2,1,0:T(8,128)}, f32[4,32,256]{2,1,0:T(8,128)S(1)}, u32[]{:S(2)}, u32[]{:S(2)}) collective-permute-start(f32[4,32,256]{2,1,0:T(8,128)} %get-tuple-element.17), channel_id=1, source_target_pairs={{1,2},{2,1},{3,4},{4,3},{5,6},{6,5},{7,8},{8,7},{9,10},{10,9},{11,... | collective-permute-start | bytes 393224 | tf_op jit(solution)/shard_map/ppermute | solution.py:590
  13.9 10.8 %all-to-all-start = ((f32[128,1,128]{2,1,0:T(1,128)}), f32[128,1,128]{2,1,0:T(1,128)S(1)}, u32[]{:S(2)}, u32[]{:S(2)}) async-start(f32[128,1,128]{2,1,0:T(1,128)} %bitcast.8), calls=%async_computation | async-start | bytes 131072 | tf_op jit(solution)/shard_map/all_to_all | solution.py:580
  24.7 0.0 collective-permute-done.2.got_sa
  24.7 0.0 collective-permute-done.3.got_sb
  24.7 0.0 collective-permute-done.got_pa
  24.7 0.0 collective-permute-done.1.got_pb
  24.7 0.0 copy-done.5
  24.8 0.0 copy-done.1
  24.8 0.0 copy-done.4
  24.8 0.0 copy-start
  24.8 0.0 copy-start.2
  24.8 0.0 copy-start.3
  24.8 0.0 copy-start.6
  24.8 0.0 copy-start.7
  24.8 9.0 %stencil.1 = (f32[4,32,64,256]{3,2,1,0:T(8,128)}, f32[32,64,128]{2,1,0:T(8,128)S(1)}) custom-call(f32[4,32,64,256]{3,2,1,0:T(8,128)} %state.3, f32[32,1024,128]{2,1,0:T(8,128)} %get-tuple-element.13.force_in, f32[2,1024]{1,0:T(2,128)S(1)} %copy-done.4, s32[1,1024]{1,0:T(1,128)S(1)} %bitcast.11, f32[64,64]{1,0:T(8,128)S(1)} %copy-done.1, ...), custom_call_target="tpu_custom_call" | custom-call | bytes 30000000 | tf_op jit(solution)/shard_map/stencil/pallas_call | solution.py:592
  33.9 0.3 all-to-all-done
  34.3 2.1 %last.1 = (f32[4,32,64,256]{3,2,1,0:T(8,128)}, f32[16,2048]{1,0:T(8,128)}) custom-call(f32[4,32,64,256]{3,2,1,0:T(8,128)} %get-tuple-element.18.state, f32[32,64,128]{2,1,0:T(8,128)S(1)} %get-tuple-element.19.kept, f32[128,128]{1,0:T(8,128)S(1)} %bitcast.9, f32[128,128]{1,0:T(8,128)S(1)} %copy-done.2, ...), custom_call_target="tpu_custom_call", output_to_operand_aliasing={{0}: (0, {})} | custom-call | bytes 9000000 | tf_op jit(solution)/shard_map/last/pallas_call | solution.py:611
  (9 shorter events, 0.0 us)
Async XLA Ops:
  0.6 24.1 %copy-start.5 = (s32[1024]{0:T(1024)S(1)}, s32[1024]{0:T(1024)}, u32[]{:S(2)}) copy-start(s32[1024]{0:T(1024)} %param.17) | copy-start | bytes 12292
  0.6 24.1 %copy-start.1 = (f32[64,64]{1,0:T(8,128)S(1)}, f32[64,64]{1,0:T(8,128)}, u32[]{:S(2)}) copy-start(f32[64,64]{1,0:T(8,128)} %wall_inv.3) | copy-start | bytes 49156
  0.7 24.1 %copy-start.4 = (f32[2,1024]{1,0:T(2,128)S(1)}, f32[2,1024]{1,0:T(2,128)}, u32[]{:S(2)}) copy-start(f32[2,1024]{1,0:T(2,128)} %coef.3) | copy-start | bytes 24580
  8.8 15.9 %collective-permute-start = (f32[4,64,256]{2,1,0:T(8,128)}, f32[4,64,256]{2,1,0:T(8,128)S(1)}, u32[]{:S(2)}, u32[]{:S(2)}) collective-permute-start(f32[4,64,256]{2,1,0:T(8,128)} %get-tuple-element.14), channel_id=1, source_target_pairs={{0,16},{16,0},{32,48},{48,32},{64,80},{80,64},{96,112},{112,96},{1... | collective-permute-start | bytes 786440 | tf_op jit(solution)/shard_map/ppermute | solution.py:587
  10.3 14.4 %collective-permute-start.1 = (f32[4,64,256]{2,1,0:T(8,128)}, f32[4,64,256]{2,1,0:T(8,128)S(1)}, u32[]{:S(2)}, u32[]{:S(2)}) collective-permute-start(f32[4,64,256]{2,1,0:T(8,128)} %get-tuple-element.15), channel_id=1, source_target_pairs={{0,112},{16,32},{32,16},{48,64},{64,48},{80,96},{96,80},{112,0},{1... | collective-permute-start | bytes 786440 | tf_op jit(solution)/shard_map/ppermute | solution.py:588
  11.6 13.1 %collective-permute-start.2 = (f32[4,32,256]{2,1,0:T(8,128)}, f32[4,32,256]{2,1,0:T(8,128)S(1)}, u32[]{:S(2)}, u32[]{:S(2)}) collective-permute-start(f32[4,32,256]{2,1,0:T(8,128)} %get-tuple-element.16), channel_id=1, source_target_pairs={{0,1},{1,0},{2,3},{3,2},{4,5},{5,4},{6,7},{7,6},{8,9},{9,8},{10,11... | collective-permute-start | bytes 393224 | tf_op jit(solution)/shard_map/ppermute | solution.py:589
  13.3 11.4 %collective-permute-start.3 = (f32[4,32,256]{2,1,0:T(8,128)}, f32[4,32,256]{2,1,0:T(8,128)S(1)}, u32[]{:S(2)}, u32[]{:S(2)}) collective-permute-start(f32[4,32,256]{2,1,0:T(8,128)} %get-tuple-element.17), channel_id=1, source_target_pairs={{1,2},{2,1},{3,4},{4,3},{5,6},{6,5},{7,8},{8,7},{9,10},{10,9},{11,... | collective-permute-start | bytes 393224 | tf_op jit(solution)/shard_map/ppermute | solution.py:590
  13.9 20.3 %all-to-all-start = ((f32[128,1,128]{2,1,0:T(1,128)}), f32[128,1,128]{2,1,0:T(1,128)S(1)}, u32[]{:S(2)}, u32[]{:S(2)}) async-start(f32[128,1,128]{2,1,0:T(1,128)} %bitcast.8), calls=%async_computation | async-start | bytes 131072 | tf_op jit(solution)/shard_map/all_to_all | solution.py:580
  24.8 9.5 %copy-start = (f32[16,2048]{1,0:T(8,128)S(1)}, f32[16,2048]{1,0:T(8,128)}, u32[]{:S(2)}) copy-start(f32[16,2048]{1,0:T(8,128)} %metal.1) | copy-start | bytes 393220
  24.8 9.5 %copy-start.2 = (f32[128,128]{1,0:T(8,128)S(1)}, f32[128,128]{1,0:T(8,128)}, u32[]{:S(2)}) copy-start(f32[128,128]{1,0:T(8,128)} %get-tuple-element.20.send) | copy-start | bytes 196612
  24.8 9.5 %copy-start.3 = (f32[16,2048]{1,0:T(8,128)S(1)}, f32[16,2048]{1,0:T(8,128)}, u32[]{:S(2)}) copy-start(f32[16,2048]{1,0:T(8,128)} %get-tuple-element.21.free) | copy-start | bytes 393220
  24.8 9.4 %copy-start.6 = (f32[16,16]{1,0:T(8,128)S(1)}, f32[16,16]{1,0:T(8,128)}, u32[]{:S(2)}) copy-start(f32[16,16]{1,0:T(8,128)} %metal_inv.1) | copy-start | bytes 3076
  24.8 9.4 %copy-start.7 = (s32[1024,1]{0,1:T(1,128)S(1)}, s32[1024,1]{0,1:T(1,128)}, u32[]{:S(2)}) copy-start(s32[1024,1]{0,1:T(1,128)} %param.16) | copy-start | bytes 12292
  24.8 9.4 %copy-start.8 = (s32[1,1024]{1,0:T(1,128)S(1)}, s32[1,1024]{1,0:T(1,128)}, u32[]{:S(2)}) copy-start(s32[1,1024]{1,0:T(1,128)} %get-tuple-element.22.rank) | copy-start | bytes 12292
  24.8 9.4 %copy-start.9 = (f32[1,1024]{1,0:T(1,128)S(1)}, f32[1,1024]{1,0:T(1,128)}, u32[]{:S(2)}) copy-start(f32[1,1024]{1,0:T(1,128)} %get-tuple-element.23.top) | copy-start | bytes 12292

commit v3 on v2

--- a/solution.py
+++ b/solution.py
@@ -170,10 +170,31 @@
         temp[pl.ds(base, 8), :] = picked[2]
         return 0
 
-    lax.fori_loop(0, FACES // 8, body, 0, unroll=8)
+    lax.fori_loop(0, FACES // 8, body, 0, unroll=16)
 
     give = [pltpu.make_async_copy(force, force_out.at[0], sems.at[11])]
     give[0].start()
+
+    for copy in loads[6:] + edges_in:
+        copy.wait()
+    edges_out = [
+        pltpu.make_async_copy(edge_p.at[0], give_pa, sems.at[4]),
+        pltpu.make_async_copy(edge_p.at[1], give_pb, sems.at[5]),
+    ]
+    for copy in edges_out:
+        copy.start()
+    for c in range(4):
+        for h in range(2):
+            lanes = slice(128 * h, 128 * h + 128)
+            for p in range(0, CP, 8):
+                for k, row in enumerate(((1 - odd_s) * (CS - 1), odd_s * (CS - 1))):
+                    edge_s[k, c, p : p + 8, lanes] = halves[c][h][
+                        pl.ds(p * CS + row, 8, stride=CS), :
+                    ]
+    give.append(pltpu.make_async_copy(edge_s.at[0], give_sa, sems.at[7]))
+    give.append(pltpu.make_async_copy(edge_s.at[1], give_sb, sems.at[8]))
+    give[-1].start()
+    give[-2].start()
 
     g = wall_inv[...]
     g_hi, g_lo = split2(g)
@@ -205,28 +226,7 @@
     total = total + pltpu.roll(total, 96, 1) + pltpu.roll(total, 64, 1)
     out_send[...] = jnp.where(lane < 32, own_half, jnp.where(lane < 64, total, 0.0))
     give.append(pltpu.make_async_copy(out_send, send, sems.at[6]))
-    give[1].start()
-
-    for copy in loads[6:] + edges_in:
-        copy.wait()
-    edges_out = [
-        pltpu.make_async_copy(edge_p.at[0], give_pa, sems.at[4]),
-        pltpu.make_async_copy(edge_p.at[1], give_pb, sems.at[5]),
-    ]
-    for copy in edges_out:
-        copy.start()
-    for c in range(4):
-        for h in range(2):
-            lanes = slice(128 * h, 128 * h + 128)
-            for p in range(0, CP, 8):
-                for k, row in enumerate(((1 - odd_s) * (CS - 1), odd_s * (CS - 1))):
-                    edge_s[k, c, p : p + 8, lanes] = halves[c][h][
-                        pl.ds(p * CS + row, 8, stride=CS), :
-                    ]
-    give.append(pltpu.make_async_copy(edge_s.at[0], give_sa, sems.at[7]))
-    give.append(pltpu.make_async_copy(edge_s.at[1], give_sb, sems.at[8]))
     give[-1].start()
-    give[-2].start()
     for copy in edges_out + give:
         copy.wait()
 

time: 36.5 us -> 36.1 us (0.989)
  Pallas kernels: 19.3 us -> 18.8 us
    pallas_call x1, Pallas kernels: 8.11 us -> 7.67 us  [local(): pl.pallas_call(first_kernel, name='first', in_specs=[spec(HBM)] * 10, out...]
where the time goes in v3:
time: 36.1 us; the launch traced here: 36 us
  Pallas kernels  18.8 us (52%)
  starting transfers between devices  15.9 us (44%)
  between operations  0.84 us (2%)
  waiting for transfers between devices  0.38 us (1%)
    all_to_all x1, starting transfers between devices, local(): recv = lax.all_to_all(send, AXES, split_axis=0, concat_axis=0, tiled=True)  10.8 us
    pallas_call x1, Pallas kernels, local(): pl.pallas_call(stencil_kernel, name='stencil', in_specs=[spec(ANY), spec(...  9.01 us
    pallas_call x1, Pallas kernels, local(): pl.pallas_call(first_kernel, name='first', in_specs=[spec(HBM)] * 10, out...  7.67 us
    pallas_call x1, Pallas kernels, local(): pl.pallas_call(last_kernel, name='last', in_specs=[spec(ANY)] + [spec(VM)...  2.11 us
    ppermute x1, starting transfers between devices, local(): got_sa = lax.ppermute(give_sa, 'span', within_s)  1.65 us
    ppermute x1, starting transfers between devices, local(): got_pa = lax.ppermute(give_pa, 'pitch', within_p)  1.5 us
    ppermute x1, starting transfers between devices, local(): got_pb = lax.ppermute(give_pb, 'pitch', across_p)  1.35 us
  transfers between devices with their start and end apart: 5, of which 1 were waited for; matrix products, arithmetic and copies ran while one was open for 0% of the time, Pallas kernels for 25%

profile of v3, /device:TPU:1, one launch (start us, length us, event | category | flops | bytes accessed | tf_op | source)
XLA Modules:
  0.0 36.0 jit_solution(4637120577407783031)
XLA Ops:
  0.6 0.0 copy-start.5
  0.6 0.0 copy-start.1
  0.7 0.0 copy-start.4
  0.7 7.7 %first.1 = (f32[128,128]{1,0:T(8,128)}, f32[4,64,256]{2,1,0:T(8,128)}, f32[4,64,256]{2,1,0:T(8,128)}, f32[4,32,256]{2,1,0:T(8,128)}, f32[4,32,256]{2,1,0:T(8,128...) custom-call(f32[4,32,64,256]{3,2,1,0:T(8,128)} %state.3, ...), custom_call_target="tpu_custom_call" | custom-call | bytes 21000000 | tf_op jit(solution)/shard_map/first/pallas_call | solution.py:538
  8.3 1.5 %collective-permute-start = (f32[4,64,256]{2,1,0:T(8,128)}, f32[4,64,256]{2,1,0:T(8,128)S(1)}, u32[]{:S(2)}, u32[]{:S(2)}) collective-permute-start(f32[4,64,256]{2,1,0:T(8,128)} %get-tuple-element.14), channel_id=1, source_target_pairs={{0,16},{16,0},{32,48},{48,32},{64,80},{80,64},{96,112},{112,96},{1... | collective-permute-start | bytes 786440 | tf_op jit(solution)/shard_map/ppermute | solution.py:587
  9.8 1.4 %collective-permute-start.1 = (f32[4,64,256]{2,1,0:T(8,128)}, f32[4,64,256]{2,1,0:T(8,128)S(1)}, u32[]{:S(2)}, u32[]{:S(2)}) collective-permute-start(f32[4,64,256]{2,1,0:T(8,128)} %get-tuple-element.15), channel_id=1, source_target_pairs={{0,112},{16,32},{32,16},{48,64},{64,48},{80,96},{96,80},{112,0},{1... | collective-permute-start | bytes 786440 | tf_op jit(solution)/shard_map/ppermute | solution.py:588
  11.2 1.6 %collective-permute-start.2 = (f32[4,32,256]{2,1,0:T(8,128)}, f32[4,32,256]{2,1,0:T(8,128)S(1)}, u32[]{:S(2)}, u32[]{:S(2)}) collective-permute-start(f32[4,32,256]{2,1,0:T(8,128)} %get-tuple-element.16), channel_id=1, source_target_pairs={{0,1},{1,0},{2,3},{3,2},{4,5},{5,4},{6,7},{7,6},{8,9},{9,8},{10,11... | collective-permute-start | bytes 393224 | tf_op jit(solution)/shard_map/ppermute | solution.py:589
  12.8 0.7 %collective-permute-start.3 = (f32[4,32,256]{2,1,0:T(8,128)}, f32[4,32,256]{2,1,0:T(8,128)S(1)}, u32[]{:S(2)}, u32[]{:S(2)}) collective-permute-start(f32[4,32,256]{2,1,0:T(8,128)} %get-tuple-element.17), channel_id=1, source_target_pairs={{1,2},{2,1},{3,4},{4,3},{5,6},{6,5},{7,8},{8,7},{9,10},{10,9},{11,... | collective-permute-start | bytes 393224 | tf_op jit(solution)/shard_map/ppermute | solution.py:590
  13.5 10.8 %all-to-all-start = ((f32[128,1,128]{2,1,0:T(1,128)}), f32[128,1,128]{2,1,0:T(1,128)S(1)}, u32[]{:S(2)}, u32[]{:S(2)}) async-start(f32[128,1,128]{2,1,0:T(1,128)} %bitcast.8), calls=%async_computation | async-start | bytes 131072 | tf_op jit(solution)/shard_map/all_to_all | solution.py:580
  24.3 0.0 collective-permute-done.2.got_sa
  24.3 0.0 collective-permute-done.3.got_sb
  24.3 0.0 collective-permute-done.got_pa
  24.3 0.0 collective-permute-done.1.got_pb
  24.3 0.0 copy-done.5
  24.3 0.0 copy-done.1
  24.3 0.0 copy-done.4
  24.3 0.0 copy-start
  24.4 0.0 copy-start.2
  24.4 0.0 copy-start.6
  24.4 0.0 copy-start.7
  24.4 9.0 %stencil.1 = (f32[4,32,64,256]{3,2,1,0:T(8,128)}, f32[32,64,128]{2,1,0:T(8,128)S(1)}) custom-call(f32[4,32,64,256]{3,2,1,0:T(8,128)} %state.3, f32[32,1024,128]{2,1,0:T(8,128)} %get-tuple-element.13.force_in, f32[2,1024]{1,0:T(2,128)S(1)} %copy-done.4, s32[1,1024]{1,0:T(1,128)S(1)} %bitcast.11, f32[64,64]{1,0:T(8,128)S(1)} %copy-done.1, ...), custom_call_target="tpu_custom_call" | custom-call | bytes 30000000 | tf_op jit(solution)/shard_map/stencil/pallas_call | solution.py:592
  33.4 0.4 %all-to-all-done = f32[128,1,128]{2,1,0:T(1,128)S(1)} async-done(((f32[128,1,128]{2,1,0:T(1,128)}), f32[128,1,128]{2,1,0:T(1,128)S(1)}, u32[]{:S(2)}, u32[]{:S(2)}) %all-to-all-start) | async-done | bytes 65568 | tf_op jit(solution)/shard_map/all_to_all | solution.py:580
  33.8 0.0 copy-done.2
  33.9 2.1 %last.1 = (f32[4,32,64,256]{3,2,1,0:T(8,128)}, f32[16,2048]{1,0:T(8,128)}) custom-call(f32[4,32,64,256]{3,2,1,0:T(8,128)} %get-tuple-element.18.state, f32[32,64,128]{2,1,0:T(8,128)S(1)} %get-tuple-element.19.kept, f32[128,128]{1,0:T(8,128)S(1)} %bitcast.9, f32[128,128]{1,0:T(8,128)S(1)} %copy-done.2, ...), custom_call_target="tpu_custom_call", output_to_operand_aliasing={{0}: (0, {})} | custom-call | bytes 9000000 | tf_op jit(solution)/shard_map/last/pallas_call | solution.py:611
  (9 shorter events, 0.0 us)
Async XLA Ops:
  0.6 23.7 %copy-start.5 = (s32[1024]{0:T(1024)S(1)}, s32[1024]{0:T(1024)}, u32[]{:S(2)}) copy-start(s32[1024]{0:T(1024)} %param.17) | copy-start | bytes 12292
  0.6 23.7 %copy-start.1 = (f32[64,64]{1,0:T(8,128)S(1)}, f32[64,64]{1,0:T(8,128)}, u32[]{:S(2)}) copy-start(f32[64,64]{1,0:T(8,128)} %wall_inv.3) | copy-start | bytes 49156
  0.7 23.7 %copy-start.4 = (f32[2,1024]{1,0:T(2,128)S(1)}, f32[2,1024]{1,0:T(2,128)}, u32[]{:S(2)}) copy-start(f32[2,1024]{1,0:T(2,128)} %coef.3) | copy-start | bytes 24580
  8.3 16.0 %collective-permute-start = (f32[4,64,256]{2,1,0:T(8,128)}, f32[4,64,256]{2,1,0:T(8,128)S(1)}, u32[]{:S(2)}, u32[]{:S(2)}) collective-permute-start(f32[4,64,256]{2,1,0:T(8,128)} %get-tuple-element.14), channel_id=1, source_target_pairs={{0,16},{16,0},{32,48},{48,32},{64,80},{80,64},{96,112},{112,96},{1... | collective-permute-start | bytes 786440 | tf_op jit(solution)/shard_map/ppermute | solution.py:587
  9.8 14.5 %collective-permute-start.1 = (f32[4,64,256]{2,1,0:T(8,128)}, f32[4,64,256]{2,1,0:T(8,128)S(1)}, u32[]{:S(2)}, u32[]{:S(2)}) collective-permute-start(f32[4,64,256]{2,1,0:T(8,128)} %get-tuple-element.15), channel_id=1, source_target_pairs={{0,112},{16,32},{32,16},{48,64},{64,48},{80,96},{96,80},{112,0},{1... | collective-permute-start | bytes 786440 | tf_op jit(solution)/shard_map/ppermute | solution.py:588
  11.2 13.1 %collective-permute-start.2 = (f32[4,32,256]{2,1,0:T(8,128)}, f32[4,32,256]{2,1,0:T(8,128)S(1)}, u32[]{:S(2)}, u32[]{:S(2)}) collective-permute-start(f32[4,32,256]{2,1,0:T(8,128)} %get-tuple-element.16), channel_id=1, source_target_pairs={{0,1},{1,0},{2,3},{3,2},{4,5},{5,4},{6,7},{7,6},{8,9},{9,8},{10,11... | collective-permute-start | bytes 393224 | tf_op jit(solution)/shard_map/ppermute | solution.py:589
  12.8 11.4 %collective-permute-start.3 = (f32[4,32,256]{2,1,0:T(8,128)}, f32[4,32,256]{2,1,0:T(8,128)S(1)}, u32[]{:S(2)}, u32[]{:S(2)}) collective-permute-start(f32[4,32,256]{2,1,0:T(8,128)} %get-tuple-element.17), channel_id=1, source_target_pairs={{1,2},{2,1},{3,4},{4,3},{5,6},{6,5},{7,8},{8,7},{9,10},{10,9},{11,... | collective-permute-start | bytes 393224 | tf_op jit(solution)/shard_map/ppermute | solution.py:590
  13.5 20.3 %all-to-all-start = ((f32[128,1,128]{2,1,0:T(1,128)}), f32[128,1,128]{2,1,0:T(1,128)S(1)}, u32[]{:S(2)}, u32[]{:S(2)}) async-start(f32[128,1,128]{2,1,0:T(1,128)} %bitcast.8), calls=%async_computation | async-start | bytes 131072 | tf_op jit(solution)/shard_map/all_to_all | solution.py:580
  24.3 9.5 %copy-start = (f32[16,2048]{1,0:T(8,128)S(1)}, f32[16,2048]{1,0:T(8,128)}, u32[]{:S(2)}) copy-start(f32[16,2048]{1,0:T(8,128)} %metal.1) | copy-start | bytes 393220
  24.4 9.5 %copy-start.2 = (f32[128,128]{1,0:T(8,128)S(1)}, f32[128,128]{1,0:T(8,128)}, u32[]{:S(2)}) copy-start(f32[128,128]{1,0:T(8,128)} %get-tuple-element.20.send) | copy-start | bytes 196612
  24.4 9.5 %copy-start.3 = (f32[16,2048]{1,0:T(8,128)S(1)}, f32[16,2048]{1,0:T(8,128)}, u32[]{:S(2)}) copy-start(f32[16,2048]{1,0:T(8,128)} %get-tuple-element.21.free) | copy-start | bytes 393220
  24.4 9.4 %copy-start.6 = (f32[16,16]{1,0:T(8,128)S(1)}, f32[16,16]{1,0:T(8,128)}, u32[]{:S(2)}) copy-start(f32[16,16]{1,0:T(8,128)} %metal_inv.1) | copy-start | bytes 3076
  24.4 9.4 %copy-start.7 = (s32[1024,1]{0,1:T(1,128)S(1)}, s32[1024,1]{0,1:T(1,128)}, u32[]{:S(2)}) copy-start(s32[1024,1]{0,1:T(1,128)} %param.16) | copy-start | bytes 12292
  24.4 9.4 %copy-start.8 = (s32[1,1024]{1,0:T(1,128)S(1)}, s32[1,1024]{1,0:T(1,128)}, u32[]{:S(2)}) copy-start(s32[1,1024]{1,0:T(1,128)} %get-tuple-element.22.rank) | copy-start | bytes 12292
  24.4 9.4 %copy-start.9 = (f32[1,1024]{1,0:T(1,128)S(1)}, f32[1,1024]{1,0:T(1,128)}, u32[]{:S(2)}) copy-start(f32[1,1024]{1,0:T(1,128)} %get-tuple-element.23.top) | copy-start | bytes 12292

commit v4 on v3

--- a/solution.py
+++ b/solution.py
@@ -170,7 +170,7 @@
         temp[pl.ds(base, 8), :] = picked[2]
         return 0
 
-    lax.fori_loop(0, FACES // 8, body, 0, unroll=16)
+    lax.fori_loop(0, FACES // 8, body, 0, unroll=32)
 
     give = [pltpu.make_async_copy(force, force_out.at[0], sems.at[11])]
     give[0].start()

time: 36.1 us -> 36 us (level)
  no operation moved by 1% of the time
where the time goes in v4:
time: 36 us; the launch traced here: 35.8 us
  Pallas kernels  18.7 us (52%)
  starting transfers between devices  15.9 us (44%)
  between operations  0.84 us (2%)
  waiting for transfers between devices  0.36 us (1%)
    all_to_all x1, starting transfers between devices, local(): recv = lax.all_to_all(send, AXES, split_axis=0, concat_axis=0, tiled=True)  10.8 us
    pallas_call x1, Pallas kernels, local(): pl.pallas_call(stencil_kernel, name='stencil', in_specs=[spec(ANY), spec(...  9.03 us
    pallas_call x1, Pallas kernels, local(): pl.pallas_call(first_kernel, name='first', in_specs=[spec(HBM)] * 10, out...  7.52 us
    pallas_call x1, Pallas kernels, local(): pl.pallas_call(last_kernel, name='last', in_specs=[spec(ANY)] + [spec(VM)...  2.11 us
    ppermute x1, starting transfers between devices, local(): got_sa = lax.ppermute(give_sa, 'span', within_s)  1.63 us
    ppermute x1, starting transfers between devices, local(): got_pa = lax.ppermute(give_pa, 'pitch', within_p)  1.5 us
    ppermute x1, starting transfers between devices, local(): got_pb = lax.ppermute(give_pb, 'pitch', across_p)  1.36 us
  transfers between devices with their start and end apart: 5, of which 1 were waited for; matrix products, arithmetic and copies ran while one was open for 0% of the time, Pallas kernels for 25%

profile of v4, /device:TPU:1, one launch (start us, length us, event | category | flops | bytes accessed | tf_op | source)
XLA Modules:
  0.0 35.8 jit_solution(1987500936784545598)
XLA Ops:
  0.6 0.0 copy-start.5
  0.6 0.0 copy-start.1
  0.7 0.0 copy-start.4
  0.7 7.5 %first.1 = (f32[128,128]{1,0:T(8,128)}, f32[4,64,256]{2,1,0:T(8,128)}, f32[4,64,256]{2,1,0:T(8,128)}, f32[4,32,256]{2,1,0:T(8,128)}, f32[4,32,256]{2,1,0:T(8,128...) custom-call(f32[4,32,64,256]{3,2,1,0:T(8,128)} %state.3, ...), custom_call_target="tpu_custom_call" | custom-call | bytes 21000000 | tf_op jit(solution)/shard_map/first/pallas_call | solution.py:538
  8.2 1.5 %collective-permute-start = (f32[4,64,256]{2,1,0:T(8,128)}, f32[4,64,256]{2,1,0:T(8,128)S(1)}, u32[]{:S(2)}, u32[]{:S(2)}) collective-permute-start(f32[4,64,256]{2,1,0:T(8,128)} %get-tuple-element.14), channel_id=1, source_target_pairs={{0,16},{16,0},{32,48},{48,32},{64,80},{80,64},{96,112},{112,96},{1... | collective-permute-start | bytes 786440 | tf_op jit(solution)/shard_map/ppermute | solution.py:587
  9.7 1.4 %collective-permute-start.1 = (f32[4,64,256]{2,1,0:T(8,128)}, f32[4,64,256]{2,1,0:T(8,128)S(1)}, u32[]{:S(2)}, u32[]{:S(2)}) collective-permute-start(f32[4,64,256]{2,1,0:T(8,128)} %get-tuple-element.15), channel_id=1, source_target_pairs={{0,112},{16,32},{32,16},{48,64},{64,48},{80,96},{96,80},{112,0},{1... | collective-permute-start | bytes 786440 | tf_op jit(solution)/shard_map/ppermute | solution.py:588
  11.0 1.6 %collective-permute-start.2 = (f32[4,32,256]{2,1,0:T(8,128)}, f32[4,32,256]{2,1,0:T(8,128)S(1)}, u32[]{:S(2)}, u32[]{:S(2)}) collective-permute-start(f32[4,32,256]{2,1,0:T(8,128)} %get-tuple-element.16), channel_id=1, source_target_pairs={{0,1},{1,0},{2,3},{3,2},{4,5},{5,4},{6,7},{7,6},{8,9},{9,8},{10,11... | collective-permute-start | bytes 393224 | tf_op jit(solution)/shard_map/ppermute | solution.py:589
  12.7 0.7 %collective-permute-start.3 = (f32[4,32,256]{2,1,0:T(8,128)}, f32[4,32,256]{2,1,0:T(8,128)S(1)}, u32[]{:S(2)}, u32[]{:S(2)}) collective-permute-start(f32[4,32,256]{2,1,0:T(8,128)} %get-tuple-element.17), channel_id=1, source_target_pairs={{1,2},{2,1},{3,4},{4,3},{5,6},{6,5},{7,8},{8,7},{9,10},{10,9},{11,... | collective-permute-start | bytes 393224 | tf_op jit(solution)/shard_map/ppermute | solution.py:590
  13.3 10.8 %all-to-all-start = ((f32[128,1,128]{2,1,0:T(1,128)}), f32[128,1,128]{2,1,0:T(1,128)S(1)}, u32[]{:S(2)}, u32[]{:S(2)}) async-start(f32[128,1,128]{2,1,0:T(1,128)} %bitcast.8), calls=%async_computation | async-start | bytes 131072 | tf_op jit(solution)/shard_map/all_to_all | solution.py:580
  24.1 0.0 collective-permute-done.2.got_sa
  24.1 0.0 collective-permute-done.3.got_sb
  24.1 0.0 collective-permute-done.got_pa
  24.1 0.0 collective-permute-done.1.got_pb
  24.2 0.0 copy-start
  24.2 0.0 copy-start.6
  24.2 0.0 copy-start.7
  24.2 0.0 copy-start.8
  24.2 0.0 copy-start.9
  24.3 9.0 %stencil.1 = (f32[4,32,64,256]{3,2,1,0:T(8,128)}, f32[32,64,128]{2,1,0:T(8,128)S(1)}) custom-call(f32[4,32,64,256]{3,2,1,0:T(8,128)} %state.3, f32[32,1024,128]{2,1,0:T(8,128)} %get-tuple-element.13.force_in, f32[2,1024]{1,0:T(2,128)S(1)} %copy-done.4, s32[1,1024]{1,0:T(1,128)S(1)} %bitcast.11, f32[64,64]{1,0:T(8,128)S(1)} %copy-done.1, ...), custom_call_target="tpu_custom_call" | custom-call | bytes 30000000 | tf_op jit(solution)/shard_map/stencil/pallas_call | solution.py:592
  33.3 0.4 all-to-all-done
  33.7 0.0 copy-done.6
  33.7 0.0 copy-done.7
  33.7 0.0 copy-done.8
  33.7 2.1 %last.1 = (f32[4,32,64,256]{3,2,1,0:T(8,128)}, f32[16,2048]{1,0:T(8,128)}) custom-call(f32[4,32,64,256]{3,2,1,0:T(8,128)} %get-tuple-element.18.state, f32[32,64,128]{2,1,0:T(8,128)S(1)} %get-tuple-element.19.kept, f32[128,128]{1,0:T(8,128)S(1)} %bitcast.9, f32[128,128]{1,0:T(8,128)S(1)} %copy-done.2, ...), custom_call_target="tpu_custom_call", output_to_operand_aliasing={{0}: (0, {})} | custom-call | bytes 9000000 | tf_op jit(solution)/shard_map/last/pallas_call | solution.py:611
  (9 shorter events, 0.0 us)
Async XLA Ops:
  0.6 23.5 %copy-start.5 = (s32[1024]{0:T(1024)S(1)}, s32[1024]{0:T(1024)}, u32[]{:S(2)}) copy-start(s32[1024]{0:T(1024)} %param.17) | copy-start | bytes 12292
  0.6 23.5 %copy-start.1 = (f32[64,64]{1,0:T(8,128)S(1)}, f32[64,64]{1,0:T(8,128)}, u32[]{:S(2)}) copy-start(f32[64,64]{1,0:T(8,128)} %wall_inv.3) | copy-start | bytes 49156
  0.7 23.5 %copy-start.4 = (f32[2,1024]{1,0:T(2,128)S(1)}, f32[2,1024]{1,0:T(2,128)}, u32[]{:S(2)}) copy-start(f32[2,1024]{1,0:T(2,128)} %coef.3) | copy-start | bytes 24580
  8.2 15.9 %collective-permute-start = (f32[4,64,256]{2,1,0:T(8,128)}, f32[4,64,256]{2,1,0:T(8,128)S(1)}, u32[]{:S(2)}, u32[]{:S(2)}) collective-permute-start(f32[4,64,256]{2,1,0:T(8,128)} %get-tuple-element.14), channel_id=1, source_target_pairs={{0,16},{16,0},{32,48},{48,32},{64,80},{80,64},{96,112},{112,96},{1... | collective-permute-start | bytes 786440 | tf_op jit(solution)/shard_map/ppermute | solution.py:587
  9.7 14.5 %collective-permute-start.1 = (f32[4,64,256]{2,1,0:T(8,128)}, f32[4,64,256]{2,1,0:T(8,128)S(1)}, u32[]{:S(2)}, u32[]{:S(2)}) collective-permute-start(f32[4,64,256]{2,1,0:T(8,128)} %get-tuple-element.15), channel_id=1, source_target_pairs={{0,112},{16,32},{32,16},{48,64},{64,48},{80,96},{96,80},{112,0},{1... | collective-permute-start | bytes 786440 | tf_op jit(solution)/shard_map/ppermute | solution.py:588
  11.0 13.1 %collective-permute-start.2 = (f32[4,32,256]{2,1,0:T(8,128)}, f32[4,32,256]{2,1,0:T(8,128)S(1)}, u32[]{:S(2)}, u32[]{:S(2)}) collective-permute-start(f32[4,32,256]{2,1,0:T(8,128)} %get-tuple-element.16), channel_id=1, source_target_pairs={{0,1},{1,0},{2,3},{3,2},{4,5},{5,4},{6,7},{7,6},{8,9},{9,8},{10,11... | collective-permute-start | bytes 393224 | tf_op jit(solution)/shard_map/ppermute | solution.py:589
  12.7 11.4 %collective-permute-start.3 = (f32[4,32,256]{2,1,0:T(8,128)}, f32[4,32,256]{2,1,0:T(8,128)S(1)}, u32[]{:S(2)}, u32[]{:S(2)}) collective-permute-start(f32[4,32,256]{2,1,0:T(8,128)} %get-tuple-element.17), channel_id=1, source_target_pairs={{1,2},{2,1},{3,4},{4,3},{5,6},{6,5},{7,8},{8,7},{9,10},{10,9},{11,... | collective-permute-start | bytes 393224 | tf_op jit(solution)/shard_map/ppermute | solution.py:590
  13.3 20.3 %all-to-all-start = ((f32[128,1,128]{2,1,0:T(1,128)}), f32[128,1,128]{2,1,0:T(1,128)S(1)}, u32[]{:S(2)}, u32[]{:S(2)}) async-start(f32[128,1,128]{2,1,0:T(1,128)} %bitcast.8), calls=%async_computation | async-start | bytes 131072 | tf_op jit(solution)/shard_map/all_to_all | solution.py:580
  24.2 9.5 %copy-start = (f32[16,2048]{1,0:T(8,128)S(1)}, f32[16,2048]{1,0:T(8,128)}, u32[]{:S(2)}) copy-start(f32[16,2048]{1,0:T(8,128)} %metal.1) | copy-start | bytes 393220
  24.2 9.5 %copy-start.2 = (f32[128,128]{1,0:T(8,128)S(1)}, f32[128,128]{1,0:T(8,128)}, u32[]{:S(2)}) copy-start(f32[128,128]{1,0:T(8,128)} %get-tuple-element.20.send) | copy-start | bytes 196612
  24.2 9.5 %copy-start.3 = (f32[16,2048]{1,0:T(8,128)S(1)}, f32[16,2048]{1,0:T(8,128)}, u32[]{:S(2)}) copy-start(f32[16,2048]{1,0:T(8,128)} %get-tuple-element.21.free) | copy-start | bytes 393220
  24.2 9.4 %copy-start.6 = (f32[16,16]{1,0:T(8,128)S(1)}, f32[16,16]{1,0:T(8,128)}, u32[]{:S(2)}) copy-start(f32[16,16]{1,0:T(8,128)} %metal_inv.1) | copy-start | bytes 3076
  24.2 9.4 %copy-start.7 = (s32[1024,1]{0,1:T(1,128)S(1)}, s32[1024,1]{0,1:T(1,128)}, u32[]{:S(2)}) copy-start(s32[1024,1]{0,1:T(1,128)} %param.16) | copy-start | bytes 12292
  24.2 9.4 %copy-start.8 = (s32[1,1024]{1,0:T(1,128)S(1)}, s32[1,1024]{1,0:T(1,128)}, u32[]{:S(2)}) copy-start(s32[1,1024]{1,0:T(1,128)} %get-tuple-element.22.rank) | copy-start | bytes 12292
  24.2 9.4 %copy-start.9 = (f32[1,1024]{1,0:T(1,128)S(1)}, f32[1,1024]{1,0:T(1,128)}, u32[]{:S(2)}) copy-start(f32[1,1024]{1,0:T(1,128)} %get-tuple-element.23.top) | copy-start | bytes 12292
